TPU v7x, 256 devices: a whole 4x4x8 slice. The times are simulated.
256 devices in a mesh: row: 32 (over z_hi, y, core), chan: 8 (over z_lo, x).
Axes of the slice: x: 4, y: 4, z: 8 (z_hi: 4, z_lo: 2; z = z_hi * 2 + z_lo), core: 2. Of those that a mesh axis runs over, the one named last changes fastest.
Arguments:
- pair_input: bfloat16 [768, 768, 128], P('row', 'chan'), may hold values from -6 to 6
- token_valid: int32 [768], replicated, may hold values from 0 to 1, as said below
- left_proj: bfloat16 [128, 128], replicated, may hold values from -0.5 to 0.5
- left_gate: bfloat16 [128, 128], replicated, may hold values from -0.5 to 0.5
- right_proj: bfloat16 [128, 128], replicated, may hold values from -0.5 to 0.5
- right_gate: bfloat16 [128, 128], replicated, may hold values from -0.5 to 0.5
- mult_gate: bfloat16 [128, 128], replicated, may hold values from -0.5 to 0.5
- mult_out: bfloat16 [128, 128], replicated, may hold values from -1 to 1
- query_weight: bfloat16 [128, 128], replicated, may hold values from -0.5 to 0.5
- key_weight: bfloat16 [128, 128], replicated, may hold values from -0.5 to 0.5
- value_weight: bfloat16 [128, 128], replicated, may hold values from -0.5 to 0.5
- bias_weight: bfloat16 [128, 4], replicated, may hold values from -64 to 64
- heads_gate: bfloat16 [128, 128], replicated, may hold values from -0.5 to 0.5
- heads_out: bfloat16 [128, 128], replicated, may hold values from -2 to 2
- swish_in: bfloat16 [128, 512], replicated, may hold values from -0.5 to 0.5
- linear_in: bfloat16 [128, 512], replicated, may hold values from -0.5 to 0.5
- project_out: bfloat16 [512, 128], replicated, may hold values from -0.25 to 0.25
Outputs:
- pair_output: bfloat16 [768, 768, 128], P('row', 'chan')
Inputs may be any that keep to these rules, and one draw needn't show every extreme that they name: `token_valid`: 1 marks a real token and 0 padding. The crop holds four chains of 192 tokens each, every chain real up to some point and padded after it, with at least half of each chain real.
All inputs are finite; a program needn't handle non-finite values.
Results may differ from a plain program's by a relative error of at most 0.034.
The roundings to bfloat16 on the way count: a program that leaves them out, or rounds other values in their place, can miss the bound.
Values may be sent and summed in bfloat16 or wider, within the bound.
A program may use at most 128 MiB of HBM per device.

v0:
```python
import math

import jax
import jax.numpy as jnp
from jax import lax
from jax.sharding import PartitionSpec as P


def layer_norm(values, dimension):
    values = values.astype(jnp.float32)
    center = jnp.mean(values, axis=dimension, keepdims=True)
    spread = jnp.mean(jnp.square(values - center), axis=dimension, keepdims=True)
    return (values - center) * lax.rsqrt(spread + 1e-05)


def project(inputs, matrix):
    return jnp.einsum("ijc,cd->ijd", inputs, matrix, preferred_element_type=jnp.float32)


def body(
    pair_input,
    token_valid,
    left_proj,
    left_gate,
    right_proj,
    right_gate,
    mult_gate,
    mult_out,
    query_weight,
    key_weight,
    value_weight,
    bias_weight,
    heads_gate,
    heads_out,
    swish_in,
    linear_in,
    project_out,
):
    row_count, column_count = (pair_input.shape[0], pair_input.shape[1])
    heads_count = bias_weight.shape[1]
    head_size = query_weight.shape[1] // heads_count
    validity = token_valid.astype(jnp.float32)
    row_valid = lax.dynamic_slice_in_dim(validity, lax.axis_index("row") * row_count, row_count)
    column_valid = lax.dynamic_slice_in_dim(
        validity, lax.axis_index("chan") * column_count, column_count
    )
    pair_mask = row_valid[:, None] * column_valid[None, :]
    normed = layer_norm(pair_input, 2).astype(jnp.bfloat16)

    def channel_first(matrix):
        return jnp.einsum("ijc,cd->dij", normed, matrix, preferred_element_type=jnp.float32)

    left_side = (
        pair_mask * jax.nn.sigmoid(channel_first(left_gate)) * channel_first(left_proj)
    ).astype(jnp.bfloat16)
    right_side = (
        pair_mask * jax.nn.sigmoid(channel_first(right_gate)) * channel_first(right_proj)
    ).astype(jnp.bfloat16)
    left_moved, right_moved = (
        lax.all_to_all(left_side, "chan", split_axis=0, concat_axis=2, tiled=True),
        lax.all_to_all(right_side, "chan", split_axis=0, concat_axis=2, tiled=True),
    )
    product = jnp.einsum(
        "cik,cjk->cij",
        left_moved,
        lax.all_gather(right_moved, "row", axis=1, tiled=True),
        preferred_element_type=jnp.float32,
    )
    product = lax.all_to_all(product, "chan", split_axis=2, concat_axis=0, tiled=True)
    product_norm = layer_norm(product, 0).astype(jnp.bfloat16)
    update = jax.nn.sigmoid(project(normed, mult_gate)) * jnp.einsum(
        "cij,cd->ijd", product_norm, mult_out, preferred_element_type=jnp.float32
    )
    after_mult = (pair_input.astype(jnp.float32) + update).astype(jnp.bfloat16)
    normed = layer_norm(after_mult, 2).astype(jnp.bfloat16)
    queries = (
        project(normed, query_weight)
        .astype(jnp.bfloat16)
        .reshape(row_count, column_count, heads_count, head_size)
    )
    gate_value = jax.nn.sigmoid(project(normed, heads_gate))
    local_bias = jnp.einsum("jkc,ch->hjk", normed, bias_weight, preferred_element_type=jnp.float32)
    bias_rows = lax.all_gather(local_bias, "row", axis=1, tiled=True)
    bias_here = lax.all_to_all(bias_rows, "chan", split_axis=1, concat_axis=2, tiled=True)
    score_scale = 1.0 / math.sqrt(head_size)
    key_proj = project(normed, key_weight).astype(jnp.bfloat16)
    value_proj = project(normed, value_weight).astype(jnp.bfloat16)
    key_block = lax.all_gather(key_proj, "chan", axis=1, tiled=True)
    maxima = jnp.full((row_count, heads_count, column_count), -1e30, jnp.float32)
    key_count = key_block.shape[1]
    key_heads = key_block.reshape(row_count, key_count, heads_count, head_size)
    value_heads = lax.all_gather(value_proj, "chan", axis=1, tiled=True).reshape(
        row_count, key_count, heads_count, head_size
    )
    score = (
        jnp.einsum("ijhd,ikhd->ihjk", queries, key_heads, preferred_element_type=jnp.float32)
        * score_scale
    )
    score = score + bias_here[None]
    alive_keys = validity > 0.5
    score = jnp.where(alive_keys, score, -1e30)
    higher = jnp.maximum(maxima, jnp.max(score, axis=3))
    raised = jnp.exp(score - higher[..., None])
    totals = jnp.sum(raised, axis=3)
    accumulated = jnp.einsum(
        "ihjk,ikhd->ihjd",
        raised.astype(jnp.bfloat16),
        value_heads,
        preferred_element_type=jnp.float32,
    )
    maxima, totals, accumulated = (higher, totals, accumulated)
    attended = (
        (accumulated / totals[..., None])
        .transpose(0, 2, 1, 3)
        .reshape(row_count, column_count, heads_count * head_size)
    )
    heads = (gate_value * attended).astype(jnp.bfloat16)
    second = (after_mult.astype(jnp.float32) + project(heads, heads_out)).astype(jnp.bfloat16)
    normed = layer_norm(second, 2).astype(jnp.bfloat16)
    hidden = (jax.nn.silu(project(normed, swish_in)) * project(normed, linear_in)).astype(
        jnp.bfloat16
    )
    return (second.astype(jnp.float32) + project(hidden, project_out)).astype(jnp.bfloat16)


def solution(mesh):
    return jax.shard_map(
        body,
        mesh=mesh,
        in_specs=(
            P("row", "chan", None),
            P(),
            P(),
            P(),
            P(),
            P(),
            P(),
            P(),
            P(),
            P(),
            P(),
            P(),
            P(),
            P(),
            P(),
            P(),
            P(),
        ),
        out_specs=P("row", "chan", None),
        check_vma=False,
    )
```

profile of v0, /device:TPU:1, one launch (start us, length us, event | category | flops | bytes accessed | tf_op | source)
XLA Modules:
  0.0 451.9 jit_solution(9594660636964754551)
XLA Ops:
  6.6 0.8 convert_element_type.62
  7.5 1.3 convert_reduce_fusion.2
  8.8 1.9 fusion.48
  10.8 1.9 fusion.28
  12.7 1.0 fusion.42
  14.2 17.5 %all_to_all.69 = bf16[128,24,96]{2,1,0:T(8,128)(2,1)S(1)} all-to-all(bf16[128,24,96]{2,1,0:T(8,128)(2,1)S(1)} %copy.39), channel_id=1, replica_groups=mesh['row'=32,'chan'=8] {'chan'}, dimensions={0} | all-to-all | bytes 1179648 | tf_op jit(solution)/shard_map/all_to_all | solution.py:61
  31.6 0.5 copy.40
  32.2 1.5 all_to_all.57
  33.7 1.9 fusion.32
  35.6 1.0 fusion.43
  37.0 12.9 %all_to_all.70 = bf16[128,24,96]{2,1,0:T(8,128)(2,1)S(1)} all-to-all(bf16[128,24,96]{2,1,0:T(8,128)(2,1)S(1)} %copy.37), channel_id=1, replica_groups=mesh['row'=32,'chan'=8] {'chan'}, dimensions={0} | all-to-all | bytes 1179648 | tf_op jit(solution)/shard_map/all_to_all | solution.py:60
  49.9 0.5 copy.38
  50.4 0.6 all_to_all.53
  51.1 102.4 %all-gather.5.cloned.1.call-done = bf16[16,768,768]{2,1,0:T(8,128)(2,1)} async-done(((bf16[16,24,768]{2,1,0:T(8,128)(2,1)}), bf16[16,768,768]{2,1,0:T(8,128)(2,1)}) %all-gather.5.cloned.1.call-update) | async-done | bytes 18874384 | tf_op jit(solution)/shard_map/all_gather | solution.py:66
  153.5 8.9 %fusion.98 = f32[16,24,768]{2,1,0:T(8,128)S(1)} fusion(bf16[16,24,768]{2,1,0:T(8,128)(2,1)S(1)} %all_to_all.53, bf16[16,768,768]{2,1,0:T(8,128)(2,1)} %all-gather.5.cloned.1.call-done), kind=kOutput, calls=%fused_computation.110 | convolution fusion | flops 452984832 | bytes 20643840 | tf_op jit(solution)/shard_map/cik,cjk->cij/dot_general | solution.py:63
  162.4 5.0 %copy.41 = f32[16,24,768]{1,0,2:T(8,128)} copy(f32[16,24,768]{2,1,0:T(8,128)S(1)} %fusion.98) | data formatting | bytes 2359296 | tf_op jit(solution)/shard_map/cik,cjk->cij/dot_general | solution.py:63
  167.4 7.4 %reshape.112 = f32[8,1,36864]{2,1,0:T(1,128)} reshape(f32[768,16,24]{2,1,0:T(8,128)} %bitcast.104) | data formatting | bytes 2359296
  174.8 17.3 %all-to-all-start.2 = ((f32[8,1,36864]{2,1,0:T(1,128)}), f32[8,1,36864]{2,1,0:T(1,128)S(1)}, u32[]{:S(2)}, u32[]{:S(2)}) async-start(f32[8,1,36864]{2,1,0:T(1,128)} %reshape.112), calls=%async_computation.2 | async-start | bytes 2359296 | tf_op jit(solution)/shard_map/all_to_all | solution.py:69
  192.6 2.0 fusion.35
  194.5 13.9 %all-to-all-done.2 = f32[8,1,36864]{2,1,0:T(1,128)S(1)} async-done(((f32[8,1,36864]{2,1,0:T(1,128)}), f32[8,1,36864]{2,1,0:T(1,128)S(1)}, u32[]{:S(2)}, u32[]{:S(2)}) %all-to-all-start.2) | async-done | bytes 1179680 | tf_op jit(solution)/shard_map/all_to_all | solution.py:69
  208.4 1.0 copy-done.2
  209.9 4.7 %reduce.2 = f32[8,36864]{1,0:T(8,128)S(1)} reduce(f32[8,1,36864]{2,1,0:T(1,128)} %copy-done.2, f32[]{:T(128)} %broadcast.140), dimensions={1}, to_apply=%all_to_all.58.reduce_sub_computation | reduce | bytes 2359300 | tf_op jit(solution)/shard_map/all_to_all | solution.py:69
  214.7 7.2 %reshape.113 = f32[768,16,24]{2,1,0:T(8,128)} reshape(f32[8,36864]{1,0:T(8,128)S(1)} %reduce.2) | data formatting | bytes 2359296
  221.8 5.0 %copy.42 = f32[16,24,8,96]{3,1,0,2:T(8,128)S(1)} copy(f32[16,24,8,96]{1,0,3,2:T(8,128)} %bitcast.105) | data formatting | bytes 2359296 | tf_op jit(solution)/shard_map/all_to_all | solution.py:69
  227.5 1.1 copy-done.3
  228.6 0.7 convert_reduce_fusion.1
  229.3 0.8 fusion.46
  230.2 1.6 convolution_bitcast_fusion
  231.9 1.8 convolution_convert_fusion.1
  233.7 1.7 convolution_convert_fusion
  235.5 47.4 %all-gather.9.cloned.1.call-done = f32[4,768,96]{2,0,1:T(4,128)} async-done(((f32[4,24,96]{2,0,1:T(4,128)}), f32[4,768,96]{2,0,1:T(4,128)}) %all-gather.9.cloned.1.call-update) | async-done | bytes 1179664 | tf_op jit(solution)/shard_map/all_gather | solution.py:83
  282.9 4.5 all-to-all-start.3
  287.4 1.0 convolution_convert_fusion.2
  288.8 29.2 %all-to-all-done.3 = f32[4,768,96]{2,0,1:T(4,128)} async-done(((f32[4,768,96]{2,0,1:T(4,128)}), f32[4,768,96]{2,0,1:T(4,128)}, u32[]{:S(2)}, u32[]{:S(2)}) %all-to-all-start.3) | async-done | bytes 1179680 | tf_op jit(solution)/shard_map/all_to_all | solution.py:84
  318.0 3.5 copy.46
  321.5 1.9 add.86
  323.4 31.0 %all-gather.7.cloned.1.call-done = bf16[24,768,128]{2,1,0:T(8,128)(2,1)} async-done(((bf16[24,96,128]{2,1,0:T(8,128)(2,1)}), bf16[24,768,128]{2,1,0:T(8,128)(2,1)}) %all-gather.7.cloned.1.call-update) | async-done | bytes 4718608 | tf_op jit(solution)/shard_map/all_gather | solution.py:88
  354.4 6.7 %copy.45 = bf16[24,768,128]{1,2,0:T(8,128)(2,1)} copy(bf16[24,768,128]{2,1,0:T(8,128)(2,1)} %all-gather.7.cloned.1.call-done) | data formatting | bytes 9437184 | tf_op jit(solution)/shard_map/all_gather | solution.py:88
  361.0 14.2 %fusion.2 = (f32[24,4,96]{2,1,0:T(4,128)S(1)}, f32[24,4,96,768]{3,2,1,0:T(8,128)}) fusion(f32[4,96,768]{2,1,0:T(8,128)S(1)} %add.86, pred[768]{0:T(1024)(128)(4,1)S(1)} %broadcast_compare_fusion, bf16[24,96,4,32]{1,3,2,0:T(8,128)(2,1)S(1)} %bitcast.106, bf16[24,768,4,32]{1,3,2,0:T(8,128)(2,1)} %bitcast.103), kind=kOutput, calls=%fused_computation.4 | convolution fusion | flops 481287168 | bytes 34837248 | tf_op jit(solution)/shard_map/ijhd,ikhd->ihjk/dot_general | solution.py:96
  375.3 14.5 %fusion = f32[24,4,96]{2,1,0:T(4,128)} fusion(f32[24,4,96,768]{3,2,1,0:T(8,128)} %get-tuple-element.8, f32[24,4,96]{2,1,0:T(4,128)S(1)} %broadcast_maximum_fusion, f32[4,96,768]{2,1,0:T(8,128)S(1)} %add.86, pred[768]{0:T(1024)(128)(4,1)S(1)} %broadcast_compare_fusion), kind=kLoop, calls=%fused_computation.2 | loop fusion | flops 35380224 | bytes 29565696 | tf_op jit(solution)/shard_map/reduce_sum | solution.py:104
  389.8 21.3 %all-gather.11.cloned.1.call-done = bf16[24,768,128]{2,1,0:T(8,128)(2,1)} async-done(((bf16[24,96,128]{2,1,0:T(8,128)(2,1)}), bf16[24,768,128]{2,1,0:T(8,128)(2,1)}) %all-gather.11.cloned.1.call-update) | async-done | bytes 4718608 | tf_op jit(solution)/shard_map/all_gather | solution.py:92
  411.1 6.7 %copy.47 = bf16[24,768,128]{1,2,0:T(8,128)(2,1)} copy(bf16[24,768,128]{2,1,0:T(8,128)(2,1)} %all-gather.11.cloned.1.call-done) | data formatting | bytes 9437184 | tf_op jit(solution)/shard_map/all_gather | solution.py:92
  417.8 14.8 %bitcast_divide_fusion = f32[24,96,4,32]{1,3,2,0:T(8,128)S(1)} fusion(bf16[24,768,4,32]{1,3,2,0:T(8,128)(2,1)} %bitcast.107, f32[24,4,96,768]{3,2,1,0:T(8,128)} %get-tuple-element.8, f32[24,4,96]{2,1,0:T(4,128)S(1)} %broadcast_maximum_fusion, f32[4,96,768]{2,1,0:T(8,128)S(1)} %add.86, pred[768]{0:T(1024)(128)(4,1)S(1)} %broadcast_compare_fusion, ...), kind=kOutput, calls=%fused_computation.22 | convolution fusion | flops 488669184 | bytes 35463936 | tf_op jit(solution)/shard_map/ihjk,ikhd->ihjd/dot_general | solution.py:105
  432.6 1.5 copy.48
  434.0 2.4 convert_reduce_fusion
  436.5 0.8 fusion.44
  437.3 2.7 fusion.53
  440.0 5.1 %fusion.40 = bf16[24,96,128]{2,1,0:T(8,128)(2,1)} fusion(f32[24,96,512]{2,1,0:T(8,128)} %fusion.53, bf16[24,96,128]{2,1,0:T(8,128)(2,1)S(1)} %get-tuple-element.10, f32[24,96]{1,0:T(8,128)S(1)} %add_rsqrt_fusion, f32[24,96]{1,0:T(8,128)S(1)} %broadcast_multiply_fusion.1, bf16[512,128]{1,0:T(8,128)(2,1)S(1)} %copy-done.11, bf16[128,512]{1,0:T(8,128)(2,1)S(1)} %copy-done.12), kind=kOutput, calls=%fused_computation.59 | convolution fusion | flops 613122048 | bytes 6178816 | tf_op jit(solution)/shard_map/ijc,cd->ijd/dot_general | solution.py:17
  (63 shorter events, 3.4 us)
Async XLA Ops:
  6.5 430.7 %copy-start = (bf16[128,512]{1,0:T(8,128)(2,1)S(1)}, bf16[128,512]{1,0:T(8,128)(2,1)}, u32[]{:S(2)}) copy-start(bf16[128,512]{1,0:T(8,128)(2,1)} %param.31) | copy-start | bytes 393220
  6.5 4.2 copy-start.1
  6.5 4.2 copy-start.13
  6.5 146.9 %all-gather.5.cloned.1.call-start = ((), (), s32[]{:S(2)}) async-start(), calls=%async_computation.4 | async-start | bytes 19464192 | tf_op jit(solution)/shard_map/all_gather | solution.py:66
  10.8 1.9 copy-start.4
  32.1 1.5 copy-start.14
  33.7 1.9 copy-start.5
  174.8 17.8 %copy-start.15 = (bf16[128,128]{1,0:T(8,128)(2,1)S(1)}, bf16[128,128]{1,0:T(8,128)(2,1)}, u32[]{:S(2)}) copy-start(bf16[128,128]{1,0:T(8,128)(2,1)} %param.23) | copy-start | bytes 98308
  174.8 33.6 %all-to-all-start.2 = ((f32[8,1,36864]{2,1,0:T(1,128)}), f32[8,1,36864]{2,1,0:T(1,128)S(1)}, u32[]{:S(2)}, u32[]{:S(2)}) async-start(f32[8,1,36864]{2,1,0:T(1,128)} %reshape.112), calls=%async_computation.2 | async-start | bytes 2359296 | tf_op jit(solution)/shard_map/all_to_all | solution.py:69
  192.0 90.8 %all-gather.9.cloned.1.call-start = ((), (), s32[]{:S(2)}) async-start(), calls=%async_computation.6 | async-start | bytes 1622016 | tf_op jit(solution)/shard_map/all_gather | solution.py:83
  208.4 1.0 copy-start.2
  227.3 1.3 copy-start.3
  227.3 1.3 copy-start.6
  228.6 1.6 copy-start.18
  229.3 2.5 copy-start.7
  231.8 1.9 copy-start.8
  231.8 122.6 %all-gather.7.cloned.1.call-start = ((), (), s32[]{:S(2)}) async-start(), calls=%async_computation.5 | async-start | bytes 5308416 | tf_op jit(solution)/shard_map/all_gather | solution.py:88
  233.7 177.4 %all-gather.11.cloned.1.call-start = ((), (), s32[]{:S(2)}) async-start(), calls=%async_computation.7 | async-start | bytes 5308416 | tf_op jit(solution)/shard_map/all_gather | solution.py:92
  235.5 51.9 %copy-start.10 = (s32[768]{0:T(1024)S(1)}, s32[768]{0:T(1024)}, u32[]{:S(2)}) copy-start(s32[768]{0:T(1024)} %param.18) | copy-start | bytes 9220
  235.5 51.9 %copy-start.9 = (bf16[128,128]{1,0:T(8,128)(2,1)S(1)}, bf16[128,128]{1,0:T(8,128)(2,1)}, u32[]{:S(2)}) copy-start(bf16[128,128]{1,0:T(8,128)(2,1)} %param.25) | copy-start | bytes 98308
  282.9 35.1 %all-to-all-start.3 = ((f32[4,768,96]{2,0,1:T(4,128)}), f32[4,768,96]{2,0,1:T(4,128)}, u32[]{:S(2)}, u32[]{:S(2)}) async-start(f32[4,768,96]{2,0,1:T(4,128)} %all-gather.9.cloned.1.call-done), calls=%async_computation.3 | async-start | bytes 3145728 | tf_op jit(solution)/shard_map/all_to_all | solution.py:84
  432.5 1.5 copy-start.16
  432.5 1.5 copy-start.17
  437.3 2.7 copy-start.11
  437.3 2.7 copy-start.12
Sparse Core Ops, SparseCore 0:
  33.8 119.6 all-gather.4
  231.9 50.8 all-gather.8
  284.7 69.6 all-gather.6
  356.0 55.0 all-gather.10
where the time goes:
time: 460 us; the launch traced here: 452 us
  waiting for transfers between devices  245 us (53%)
  matrix products  62.7 us (14%)
  local copies, waits for them, and re-layouts  51.9 us (11%)
  blocking collectives  30.4 us (7%)
  other arithmetic  25.5 us (6%)
  starting transfers between devices  22.3 us (5%)
  between operations  13.8 us (3%)
    all_gather x1, waiting for transfers between devices, body(): lax.all_gather(right_moved, 'row', axis=1, tiled=True)  102 us
    all_gather x1, waiting for transfers between devices, body(): bias_rows = lax.all_gather(local_bias, 'row', axis=1, tiled=True)  47.4 us
    all_gather x1, waiting for transfers between devices, body(): key_block = lax.all_gather(key_proj, 'chan', axis=1, tiled=True)  31 us
    all_to_all x1, waiting for transfers between devices, body(): lax.all_to_all(bias_rows, 'chan', split_axis=1, concat_axis=2, tiled=True)  29.2 us
    all_gather x1, waiting for transfers between devices, body(): lax.all_gather(value_proj, 'chan', axis=1, tiled=True)  21.3 us
    all_to_all x1, blocking collectives, body(): lax.all_to_all(right_side, 'chan', split_axis=0, concat_axis=2, tiled=True)  17.5 us
    all_to_all x1, starting transfers between devices, body(): lax.all_to_all(product, 'chan', split_axis=2, concat_axis=0, tiled=True)  17.3 us
    unnamed x40, local copies, waits for them, and re-layouts  16.7 us
  transfers between devices with their start and end apart: 6, of which 6 were waited for; matrix products, arithmetic and copies ran while one was open for 11% of the time, Pallas kernels for 0%

commit v1 on v0

v1 whole, which is shorter than its diff:
```python
import math

import jax
import jax.numpy as jnp
from jax import lax
from jax.experimental import pallas as pl
from jax.experimental.pallas import tpu as pltpu
from jax.sharding import PartitionSpec as P

BF16 = jnp.bfloat16
F32 = jnp.float32
LOG2E = math.log2(math.e)
MESH = pl.DeviceIdType.MESH
VMEM = pl.BlockSpec(memory_space=pltpu.VMEM)
ANY = pl.BlockSpec(memory_space=pl.ANY)
LIMIT = 60 * 1024 * 1024


def normalize(values, axis):
    center = jnp.mean(values, axis=axis, keepdims=True)
    spread = jnp.mean(jnp.square(values - center), axis=axis, keepdims=True)
    return (values - center) * lax.rsqrt(spread + 1e-05)


def dot(a, b, a_dim=1, b_dim=0):
    return lax.dot_general(a, b, (((a_dim,), (b_dim,)), ((), ())), preferred_element_type=F32)


def transposed(ref):
    return ref[...].astype(F32).T.astype(BF16)


def remote(src, dst, send_sem, recv_sem, row, chan):
    return pltpu.make_async_remote_copy(
        src_ref=src,
        dst_ref=dst,
        send_sem=send_sem,
        recv_sem=recv_sem,
        device_id=(row, chan),
        device_id_type=MESH,
    )


def triangle_kernel(
    pair_ref,
    mask_ref,
    left_proj_ref,
    left_gate_ref,
    right_proj_ref,
    right_gate_ref,
    mult_gate_ref,
    mult_out_ref,
    bias_weight_ref,
    after_ref,
    normed_ref,
    bias_ref,
    left_f,
    right_f,
    send,
    mine,
    theirs,
    left_all,
    right_all,
    product,
    back,
    gate_f,
    norm_f,
    bias_f,
    send_sem,
    recv_sem,
    local_sem,
):
    rows, columns, channels = pair_ref.shape
    chips_down, chips_across = product.shape[0], product.shape[1]
    chips = chips_down * chips_across
    row, chan = lax.axis_index("row"), lax.axis_index("chan")
    core, down = row % 2, row // 2
    here = down * chips_across + chan

    weights = jnp.concatenate(
        [transposed(ref) for ref in (left_gate_ref, left_proj_ref, right_gate_ref, right_proj_ref)],
        axis=0,
    )
    pad = jnp.zeros((128 - columns, channels), BF16)

    def edges(i, carry):
        normed = normalize(pair_ref[i].astype(F32), 1).astype(BF16)
        out = dot(weights, jnp.concatenate([normed, pad], axis=0), 1, 1)
        mask = mask_ref[i]
        at = pl.ds(pl.multiple_of(i * channels, channels), channels)
        left_f[at, :] = mask * jax.nn.sigmoid(out[0:128]) * out[128:256]
        right_f[at, :] = mask * jax.nn.sigmoid(out[256:384]) * out[384:512]
        return carry

    lax.fori_loop(0, rows, edges, 0)

    def regroup(channel, carry):
        at = pl.ds(channel, rows, stride=channels)
        send[channel] = jnp.concatenate([right_f[at, :], left_f[at, :]], axis=0).astype(BF16)
        return carry

    lax.fori_loop(0, channels, regroup, 0)

    def out_copy(step):
        other = (here + step * 37) % chips
        down_to, chan_to = other // chips_across, other % chips_across
        return remote(
            send.at[other],
            mine.at[here],
            send_sem.at[0],
            recv_sem.at[0],
            down_to * 2 + core,
            chan_to,
        )

    lax.fori_loop(1, chips, lambda step, carry: (out_copy(step).start(), carry)[1], 0)
    own = pltpu.make_async_copy(send.at[here], mine.at[here], local_sem.at[0])
    own.start()

    def gates(i, carry):
        normed = normalize(pair_ref[i].astype(F32), 1).astype(BF16)
        gate_f[i] = jax.nn.sigmoid(dot(normed, mult_gate_ref[...]))
        return carry

    lax.fori_loop(0, rows, gates, 0)
    own.wait()
    arrived = mine.at[pl.ds(0, chips - 1)]
    pltpu.make_async_copy(arrived, arrived, recv_sem.at[0]).wait()
    sent = send.at[pl.ds(0, chips - 1)]
    pltpu.make_async_copy(sent, sent, send_sem.at[0]).wait()

    swap = remote(
        mine.at[:, pl.ds(0, 32), :], theirs, send_sem.at[1], recv_sem.at[1], row + 1 - 2 * core, chan
    )
    swap.start()
    for c in range(chips_across):
        lanes = pl.ds(c * 128, 128)
        for d in range(chips_down):
            left_all[pl.ds(d * 32, 32), lanes] = mine[d * chips_across + c, 16:48, :]
            right_all[d, core, :, lanes] = mine[d * chips_across + c, 0:32, :]
    swap.wait()
    for c in range(chips_across):
        lanes = pl.ds(c * 128, 128)
        for d in range(chips_down):
            right_all[d, 1 - core, :, lanes] = theirs[d * chips_across + c]
    width = 128 * chips_across
    for c in range(0, chips_across, 2):
        right = right_all[c * 2 : c * 2 + 4].reshape(256, width)
        out = dot(left_all[...], right, 1, 1).astype(BF16)
        product[:, c] = out[:, 0:128].reshape(chips_down, 32, 128)
        product[:, c + 1] = out[:, 128:256].reshape(chips_down, 32, 128)

    def back_copy(step):
        other = (here + step * 37) % chips
        down_to, chan_to = other // chips_across, other % chips_across
        return remote(
            product.at[down_to, chan_to],
            back.at[here],
            send_sem.at[2],
            recv_sem.at[2],
            down_to * 2 + core,
            chan_to,
        )

    lax.fori_loop(1, chips, lambda step, carry: (back_copy(step).start(), carry)[1], 0)
    own = pltpu.make_async_copy(product.at[down, chan], back.at[here], local_sem.at[0])
    own.start()
    own.wait()
    arrived = back.at[pl.ds(0, chips - 1)]
    pltpu.make_async_copy(arrived, arrived, recv_sem.at[2]).wait()
    pltpu.make_async_copy(arrived, arrived, send_sem.at[2]).wait()

    def total(channel, carry):
        return carry + back[channel].astype(F32)[8:32]

    zero = jnp.zeros((rows, 128), F32)
    center = lax.fori_loop(0, channels, total, zero, unroll=8) * (1.0 / channels)

    def square(channel, carry):
        return carry + jnp.square(back[channel].astype(F32)[8:32] - center)

    spread = lax.fori_loop(0, channels, square, zero, unroll=8) * (1.0 / channels)
    scale = lax.rsqrt(spread + 1e-05)

    def scaled(channel, carry):
        at = pl.ds(pl.multiple_of(channel * rows, 8), rows)
        norm_f[at, :] = (back[channel].astype(F32)[8:32] - center) * scale
        return carry

    lax.fori_loop(0, channels, scaled, 0, unroll=8)
    bias_weights = bias_weight_ref[...].astype(F32).T.astype(BF16)
    heads = bias_weights.shape[0]
    bias_weights = jnp.concatenate(
        [bias_weights.astype(F32), jnp.zeros((8 - heads, channels), F32)], axis=0
    ).astype(BF16)

    def finish(i, carry):
        product_norm = norm_f[pl.ds(i, channels, stride=rows), :].astype(BF16)
        out = dot(product_norm, mult_out_ref[...], 0, 0)
        out = jnp.concatenate([out[32 * k : 32 * k + rows] for k in range(4)], axis=0)
        after = (pair_ref[i].astype(F32) + gate_f[i] * out).astype(BF16)
        after_ref[i] = after
        normed = normalize(after.astype(F32), 1).astype(BF16)
        normed_ref[i] = normed
        at = pl.ds(pl.multiple_of(i * 8, 8), 8)
        bias_f[at, :] = dot(bias_weights, jnp.concatenate([normed, pad], axis=0), 1, 1)
        return carry

    lax.fori_loop(0, rows, finish, 0)
    for h in range(heads):
        bias_ref[h] = bias_f[pl.ds(h, rows, stride=8), :]


def gather_kernel(
    normed_ref, bias_ref, all_ref, mine_ref, theirs_ref, send_sem, recv_sem, local_sem, bias_sem
):
    row, chan = lax.axis_index("row"), lax.axis_index("chan")
    core, down = row % 2, row // 2
    downs = 16
    zone, place = chan // 4, chan % 4
    right, left = (place + 1) % 4, (place + 3) % 4
    half = normed_ref.shape[0] // 2

    def block(z, x):
        return all_ref.at[z * 4 + x]

    def first(ref):
        return ref.at[pl.ds(0, half)]

    def second(ref):
        return ref.at[pl.ds(half, half)]

    def copy(slot, src, dst, z, x):
        return remote(src, dst, send_sem.at[slot], recv_sem.at[slot], row, z * 4 + x)

    own = pltpu.make_async_copy(normed_ref, all_ref.at[chan], local_sem.at[0])
    own.start()
    here = block(zone, place)
    copies = {}

    def go(slot, src, dst, z, x):
        copies[slot] = copy(slot, src, dst, z, x)
        copies[slot].start()

    go(0, normed_ref, here, 1 - zone, place)
    go(1, normed_ref, here, zone, right)
    go(2, normed_ref, here, zone, left)

    column = row // 4
    part = (row % 4) // 2
    landing = mine_ref.at[part, chan]
    for d in range(downs):
        self_copy = jnp.logical_and(down == d, chan == column)

        @pl.when(self_copy)
        def _():
            pltpu.make_async_copy(bias_ref, landing, bias_sem.at[1]).start()

        @pl.when(jnp.logical_not(self_copy))
        def _():
            remote(bias_ref, landing, bias_sem.at[0], bias_sem.at[1], d * 2 + core, column).start()

    copies[0].wait_recv()
    across = block(1 - zone, place)
    go(3, across, across, zone, right)
    go(4, across, across, zone, left)
    copies[1].wait_recv()
    from_left = first(block(zone, left))
    go(5, from_left, from_left, zone, right)
    copies[2].wait_recv()
    from_right = second(block(zone, right))
    go(6, from_right, from_right, zone, left)

    pltpu.make_async_copy(mine_ref, mine_ref, bias_sem.at[1]).wait()
    swap = remote(
        mine_ref, theirs_ref, bias_sem.at[2], bias_sem.at[3], row + 1 - 2 * core, chan
    )
    swap.start()

    copies[3].wait_recv()
    from_left = first(block(1 - zone, left))
    go(7, from_left, from_left, zone, right)
    copies[4].wait_recv()
    from_right = second(block(1 - zone, right))
    go(8, from_right, from_right, zone, left)
    for slot in (5, 6, 7, 8):
        copies[slot].wait_recv()
    for slot in range(9):
        copies[slot].wait_send()
    own.wait()
    swap.wait()
    for d in range(downs):
        self_copy = jnp.logical_and(down == d, chan == column)

        @pl.when(jnp.logical_not(self_copy))
        def _():
            remote(
                bias_ref, landing, bias_sem.at[0], bias_sem.at[1], d * 2 + core, column
            ).wait_send()


def attention_kernel(
    core_ref,
    all_ref,
    own_ref,
    after_ref,
    mine_ref,
    theirs_ref,
    alive_ref,
    query_ref,
    key_ref,
    value_ref,
    gate_ref,
    heads_out_ref,
    swish_ref,
    linear_ref,
    project_ref,
    out_ref,
    bias_f,
    attended_f,
):
    blocks, step_rows, columns, channels = all_ref.shape
    heads, parts, part_rows, keys = bias_f.shape
    queries = parts * part_rows
    core = core_ref[0]

    @pl.when(pl.program_id(0) == 0)
    def _():
        alive = alive_ref[...] > 0.5
        for h in range(heads):
            for part in range(2):
                for ref, side in ((mine_ref, core), (theirs_ref, 1 - core)):
                    line = jnp.concatenate(
                        [ref[part, c, h][:, 0:columns] for c in range(blocks)], axis=1
                    )
                    bias_f[h, 2 * part + side] = jnp.where(alive, line * LOG2E, -1e30)

    head_of_lane = lax.broadcasted_iota(jnp.int32, (queries, channels), 1) // (channels // heads)
    scale = LOG2E / math.sqrt(channels // heads)
    key_value = jnp.concatenate([key_ref[...], value_ref[...]], axis=1)
    ones = jnp.ones((keys, channels), BF16)

    for t in range(step_rows):
        tokens = jnp.concatenate([all_ref[c, t] for c in range(blocks)], axis=0)
        projected = dot(tokens, key_value).astype(BF16)
        key, value = projected[:, 0:channels], projected[:, channels:]
        query = dot(own_ref[t], query_ref[...])
        spread = jnp.concatenate(
            [jnp.where(head_of_lane == h, query, 0.0) for h in range(heads)], axis=0
        ).astype(BF16)
        score = dot(spread, key, 1, 1) * scale + bias_f[...].reshape(heads * queries, keys)
        raised = jnp.exp2(score - jnp.max(score, axis=1, keepdims=True)).astype(BF16)
        summed = dot(raised, jnp.concatenate([value, ones], axis=1))
        top = jnp.zeros((queries, channels), F32)
        bottom = jnp.zeros((queries, channels), F32)
        for h in range(heads):
            at = slice(h * queries, (h + 1) * queries)
            top = jnp.where(head_of_lane == h, summed[at, 0:channels], top)
            bottom = jnp.where(head_of_lane == h, summed[at, channels:], bottom)
        attended_f[pl.ds(t * queries, queries), :] = top / bottom

    normed = own_ref[...].reshape(step_rows * columns, channels)
    gate = jax.nn.sigmoid(dot(normed, gate_ref[...]))
    mixed = (gate * attended_f[...]).astype(BF16)
    after = after_ref[...].reshape(step_rows * columns, channels).astype(F32)
    second = (after + dot(mixed, heads_out_ref[...])).astype(BF16)
    second_f = second.astype(F32)
    normed = normalize(second_f, 1).astype(BF16)
    hidden = (jax.nn.silu(dot(normed, swish_ref[...])) * dot(normed, linear_ref[...])).astype(BF16)
    out = (second_f + dot(hidden, project_ref[...])).astype(BF16)
    out_ref[...] = out.reshape(step_rows, columns, channels)


def body(
    pair_input,
    token_valid,
    left_proj,
    left_gate,
    right_proj,
    right_gate,
    mult_gate,
    mult_out,
    query_weight,
    key_weight,
    value_weight,
    bias_weight,
    heads_gate,
    heads_out,
    swish_in,
    linear_in,
    project_out,
):
    rows, columns, channels = pair_input.shape
    heads = bias_weight.shape[1]
    tokens = token_valid.shape[0]
    across = tokens // columns
    down = tokens // rows // 2
    chips = across * down
    row, chan = lax.axis_index("row"), lax.axis_index("chan")
    validity = token_valid.astype(F32)
    row_valid = lax.dynamic_slice_in_dim(validity, row * rows, rows)
    column_valid = lax.dynamic_slice_in_dim(validity, chan * columns, columns)
    column_valid = jnp.pad(column_valid, (0, 128 - columns))
    mask = (row_valid[:, None] * column_valid[None, :]).reshape(rows, 1, 128)

    after, normed, bias = pl.pallas_call(
        triangle_kernel,
        out_shape=[
            jax.ShapeDtypeStruct((rows, columns, channels), BF16),
            jax.ShapeDtypeStruct((rows, columns, channels), BF16),
            jax.ShapeDtypeStruct((heads, rows, 128), F32),
        ],
        in_specs=[VMEM] * 9,
        out_specs=[VMEM] * 3,
        scratch_shapes=[
            pltpu.VMEM((rows * channels, 128), F32),
            pltpu.VMEM((rows * channels, 128), F32),
            pltpu.VMEM((chips, 48, 128), BF16),
            pltpu.VMEM((chips, 48, 128), BF16),
            pltpu.VMEM((chips, 32, 128), BF16),
            pltpu.VMEM((down * 32, across * 128), BF16),
            pltpu.VMEM((down, 2, 32, across * 128), BF16),
            pltpu.VMEM((down, across, 32, 128), BF16),
            pltpu.VMEM((chips, 32, 128), BF16),
            pltpu.VMEM((rows, columns, channels), F32),
            pltpu.VMEM((channels * rows, 128), F32),
            pltpu.VMEM((rows * 8, 128), F32),
            pltpu.SemaphoreType.DMA((3,)),
            pltpu.SemaphoreType.DMA((3,)),
            pltpu.SemaphoreType.DMA((1,)),
        ],
        compiler_params=pltpu.CompilerParams(has_side_effects=True, vmem_limit_bytes=LIMIT),
        name="triangle",
    )(
        pair_input,
        mask,
        left_proj,
        left_gate,
        right_proj,
        right_gate,
        mult_gate,
        mult_out,
        bias_weight,
    )

    everything, bias_mine, bias_theirs = pl.pallas_call(
        gather_kernel,
        out_shape=[
            jax.ShapeDtypeStruct((across, rows, columns, channels), BF16),
            jax.ShapeDtypeStruct((2, across, heads, rows, 128), F32),
            jax.ShapeDtypeStruct((2, across, heads, rows, 128), F32),
        ],
        in_specs=[ANY] * 2,
        out_specs=[ANY] * 3,
        scratch_shapes=[
            pltpu.SemaphoreType.DMA((9,)),
            pltpu.SemaphoreType.DMA((9,)),
            pltpu.SemaphoreType.DMA((1,)),
            pltpu.SemaphoreType.DMA((4,)),
        ],
        compiler_params=pltpu.CompilerParams(has_side_effects=True),
        name="gather",
    )(normed, bias)

    step_rows = 4
    block = pl.BlockSpec((step_rows, columns, channels), lambda i: (i, 0, 0))
    return pl.pallas_call(
        attention_kernel,
        out_shape=jax.ShapeDtypeStruct((rows, columns, channels), BF16),
        grid=(rows // step_rows,),
        in_specs=[
            pl.BlockSpec(memory_space=pltpu.SMEM),
            pl.BlockSpec((across, step_rows, columns, channels), lambda i: (0, i, 0, 0)),
            block,
            block,
        ]
        + [VMEM] * 11,
        out_specs=block,
        scratch_shapes=[
            pltpu.VMEM((heads, 4, rows, tokens), F32),
            pltpu.VMEM((step_rows * columns, channels), F32),
        ],
        compiler_params=pltpu.CompilerParams(vmem_limit_bytes=LIMIT),
        name="attention",
    )(
        (row % 2).reshape(1).astype(jnp.int32),
        everything,
        normed,
        after,
        bias_mine,
        bias_theirs,
        validity.reshape(1, tokens),
        query_weight,
        key_weight,
        value_weight,
        heads_gate,
        heads_out,
        swish_in,
        linear_in,
        project_out,
    )


def solution(mesh):
    return jax.shard_map(
        body,
        mesh=mesh,
        in_specs=(P("row", "chan", None),) + (P(),) * 16,
        out_specs=P("row", "chan", None),
        check_vma=False,
    )
```

time: 460 us -> 210 us (0.46); the launches traced: 452 us -> 209 us
  waiting for transfers between devices: 245 us -> 0 us
  Pallas kernels: 0 us -> 206 us
  matrix products: 62.7 us -> 0 us
  local copies, waits for them, and re-layouts: 51.9 us -> 2.15 us
  blocking collectives: 30.4 us -> 0 us
  other arithmetic: 25.5 us -> 1.38 us
  starting transfers between devices: 22.3 us -> 0 us
  between operations: 13.8 us -> 0.02 us
    pallas_call x0 -> x3, Pallas kernels: none -> 206 us  [the longest x1 114 us: body(): pl.pallas_call(triangle_kernel, out_shape=[jax.ShapeDtypeStruct((rows, co...]
    all_gather x4 -> x0, waiting for transfers between devices: 202 us -> none  [the longest x1 102 us: body(): lax.all_gather(right_moved, 'row', axis=1, tiled=True)]
    dot_general x16 -> x0, matrix products: 62.7 us -> none  [the longest x7 16.7 us: project(): jnp.einsum('ijc,cd->ijd', inputs, matrix, preferred_element_type=jnp.floa...]
    all_to_all x2 -> x0, waiting for transfers between devices: 43.1 us -> none  [the longest x1 29.2 us: body(): lax.all_to_all(bias_rows, 'chan', split_axis=1, concat_axis=2, tiled=True)]
    all_to_all x2 -> x0, blocking collectives: 30.4 us -> none  [the longest x1 17.5 us: body(): lax.all_to_all(right_side, 'chan', split_axis=0, concat_axis=2, tiled=True)]
    all_to_all x2 -> x0, starting transfers between devices: 21.7 us -> none  [the longest x1 17.3 us: body(): lax.all_to_all(product, 'chan', split_axis=2, concat_axis=0, tiled=True)]
    reduce_sum x7 -> x0, other arithmetic: 19.7 us -> none  [the longest x1 14.5 us: body(): totals = jnp.sum(raised, axis=3)]
    unnamed x40 -> x1, local copies, waits for them, and re-layouts: 16.7 us -> 1.41 us
  transfers between devices with their start and end apart: 6 -> 0, of which waited for: 6 -> 0; matrix products, arithmetic and copies ran while one was open for 11% -> 0% of each run, Pallas kernels for 0% -> 0%
where the time goes in v1:
time: 210 us; the launch traced here: 209 us
  Pallas kernels  206 us (98%)
  local copies, waits for them, and re-layouts  2.15 us (1%)
    pallas_call x1, Pallas kernels, body(): pl.pallas_call(triangle_kernel, out_shape=[jax.ShapeDtypeStruct((rows, co...  114 us
    pallas_call x1, Pallas kernels, body(): pl.pallas_call(gather_kernel, out_shape=[jax.ShapeDtypeStruct((across, ro...  66.6 us
    pallas_call x1, Pallas kernels, body(): pl.pallas_call(attention_kernel, out_shape=jax.ShapeDtypeStruct((rows, co...  24.8 us

profile of v1, /device:TPU:1, one launch (start us, length us, event | category | flops | bytes accessed | tf_op | source)
XLA Modules:
  0.0 209.4 jit_solution(6567481816271793938)
XLA Ops:
  0.0 0.7 convert_element_type.5
  0.7 0.1 dynamic_slice.7
  0.8 0.1 dynamic_slice.6
  0.8 0.6 reshape.47.alive_ref
  1.4 0.7 broadcast_multiply_fusion.mask_ref
  2.1 1.4 copy.18.bias_weight_ref
  3.5 114.4 %triangle.1 = (bf16[24,96,128]{2,1,0:T(8,128)(2,1)}, bf16[24,96,128]{2,1,0:T(8,128)(2,1)}, f32[4,24,128]{2,1,0:T(8,128)}) custom-call(bf16[24,96,128]{2,1,0:T(8,128)(2,1)} %pair_ref.1, f32[24,1,128]{2,1,0:T(1,128)} %broadcast_multiply_fusion.mask_ref, bf16[128,128]{1,0:T(8,128)(2,1)} %left_proj_ref.1, bf16[128,128]{1,0:T(8,128)(2,1)} %left_gate_ref.1, ...), custom_call_target="tpu_custom_call" | custom-call | tf_op jit(solution)/shard_map/triangle/pallas_call | solution.py:406
  118.0 66.6 %gather.1 = (bf16[8,24,96,128]{3,2,1,0:T(8,128)(2,1)}, f32[2,8,4,24,128]{4,3,2,1,0:T(8,128)}, f32[2,8,4,24,128]{4,3,2,1,0:T(8,128)}) custom-call(bf16[24,96,128]{2,1,0:T(8,128)(2,1)} %get-tuple-element.11.normed_ref.own_ref, f32[4,24,128]{2,1,0:T(8,128)} %get-tuple-element.12.bias_ref), custom_call_target="tpu_custom_call" | custom-call | tf_op jit(solution)/shard_map/gather/pallas_call | solution.py:446
  184.6 24.8 %attention.1 = bf16[24,96,128]{2,1,0:T(8,128)(2,1)} custom-call(s32[1]{0:T(128)} %bitcast.core_ref, bf16[8,24,96,128]{3,2,1,0:T(8,128)(2,1)} %get-tuple-element.13.all_ref, bf16[24,96,128]{2,1,0:T(8,128)(2,1)} %get-tuple-element.11.normed_ref.own_ref, bf16[24,96,128]{2,1,0:T(8,128)(2,1)} %get-tuple-element.14.after_ref, ...), custom_call_target="tpu_custom_call" | custom-call | tf_op jit(solution)/shard_map/attention/pallas_call | solution.py:467
  (1 shorter events, 0.0 us)

commit v2 on v0

v2 whole, which is shorter than its diff:
```python
import math

import jax
import jax.numpy as jnp
from jax import lax
from jax.experimental import pallas as pl
from jax.experimental.pallas import tpu as pltpu
from jax.sharding import PartitionSpec as P

BF16 = jnp.bfloat16
F32 = jnp.float32
LOG2E = math.log2(math.e)
MESH = pl.DeviceIdType.MESH
VMEM = pl.BlockSpec(memory_space=pltpu.VMEM)
LIMIT = 60 * 1024 * 1024
GROUP = 4


def normalize(values, axis):
    center = jnp.mean(values, axis=axis, keepdims=True)
    spread = jnp.mean(jnp.square(values - center), axis=axis, keepdims=True)
    return (values - center) * lax.rsqrt(spread + 1e-05)


def dot(a, b, a_dim=1, b_dim=0):
    return lax.dot_general(a, b, (((a_dim,), (b_dim,)), ((), ())), preferred_element_type=F32)


def transposed(ref):
    return ref[...].astype(F32).T.astype(BF16)


def remote(src, dst, send_sem, recv_sem, row, chan):
    return pltpu.make_async_remote_copy(
        src_ref=src,
        dst_ref=dst,
        send_sem=send_sem,
        recv_sem=recv_sem,
        device_id=(row, chan),
        device_id_type=MESH,
    )


def block_kernel(
    pair_ref,
    mask_ref,
    alive_ref,
    left_proj_ref,
    left_gate_ref,
    right_proj_ref,
    right_gate_ref,
    mult_gate_ref,
    mult_out_ref,
    query_ref,
    key_ref,
    value_ref,
    bias_weight_ref,
    heads_gate_ref,
    heads_out_ref,
    swish_ref,
    linear_ref,
    project_ref,
    out_ref,
    left_f,
    right_f,
    normed0,
    send,
    mine,
    theirs,
    left_all,
    right_all,
    total,
    product,
    back,
    gate_f,
    norm_f,
    after_all,
    everything,
    bias_f,
    bias_send,
    bias_mine,
    bias_theirs,
    table,
    attended_f,
    edge_send,
    edge_recv,
    swap_send,
    swap_recv,
    back_send,
    back_recv,
    gather_send,
    gather_recv,
    bias_sem,
):
    rows, columns, channels = pair_ref.shape
    groups = rows // GROUP
    heads = bias_weight_ref.shape[0]
    row, chan = lax.axis_index("row"), lax.axis_index("chan")
    core, down = row % 2, row // 2
    zone, place = chan // 4, chan % 4
    here = down * 8 + chan
    pad = jnp.zeros((GROUP, 128 - columns, channels), BF16)

    def chip(step):
        dx, dz, dd = step // 32, (step // 16) % 2, step % 16
        return (down + dd) % 16, (zone + dz) % 2, (place + dx) % 4

    barrier = pltpu.get_barrier_semaphore()

    def greet(step):
        d, z, x = chip(step)
        pl.semaphore_signal(
            barrier, inc=1, device_id=(d * 2 + core, z * 4 + x), device_id_type=MESH
        )

    pl.semaphore_signal(
        barrier, inc=1, device_id=(row + 1 - 2 * core, chan), device_id_type=MESH
    )
    lax.fori_loop(1, 128, lambda step, carry: (greet(step), carry)[1], 0)

    weights = jnp.concatenate(
        [transposed(ref) for ref in (left_gate_ref, left_proj_ref, right_gate_ref, right_proj_ref)],
        axis=0,
    )

    def edges(g, carry):
        at = pl.ds(g * GROUP, GROUP)
        normed = normalize(pair_ref[at].astype(F32), 2).astype(BF16)
        normed0[at] = normed
        padded = jnp.concatenate([normed, pad], axis=1).reshape(GROUP * 128, channels)
        out = dot(weights, padded, 1, 1)
        for t in range(GROUP):
            lanes = slice(t * 128, (t + 1) * 128)
            mask = mask_ref[g * GROUP + t]
            to = pl.ds(pl.multiple_of((g * GROUP + t) * channels, channels), channels)
            left_f[to, :] = mask * jax.nn.sigmoid(out[0:128, lanes]) * out[128:256, lanes]
            right_f[to, :] = mask * jax.nn.sigmoid(out[256:384, lanes]) * out[384:512, lanes]
        return carry

    lax.fori_loop(0, groups, edges, 0)
    pl.semaphore_wait(barrier, 128)

    def edge_block(channel):
        at = pl.ds(channel, rows, stride=channels)
        return jnp.concatenate([right_f[at, :], left_f[at, :]], axis=0).astype(BF16)

    def edge_out(step, carry):
        d, z, x = chip(step)
        channel = d * 8 + z * 4 + x
        send[channel] = edge_block(channel)
        phase = step // 32
        remote(
            send.at[channel],
            mine.at[place, zone * 16 + down],
            edge_send.at[0],
            edge_recv.at[phase],
            d * 2 + core,
            z * 4 + x,
        ).start()
        return carry

    lax.fori_loop(1, 128, edge_out, 0)
    mine[place, zone * 16 + down] = edge_block(here)

    def gates(g, carry):
        at = pl.ds(g * GROUP, GROUP)
        normed = normed0[at].reshape(GROUP * columns, channels)
        gate = jax.nn.sigmoid(dot(normed, mult_gate_ref[...]))
        gate_f[at] = gate.reshape(GROUP, columns, channels)
        return carry

    lax.fori_loop(0, groups, gates, 0)

    def swap(phase):
        source = (place + 4 - phase) % 4
        return remote(
            mine.at[source, :, pl.ds(0, 32), :],
            theirs.at[source],
            swap_send.at[phase],
            swap_recv.at[phase],
            row + 1 - 2 * core,
            chan,
        )

    def arrive(phase):
        count = 31 if phase == 0 else 32
        arrived = mine.at[0, pl.ds(0, count)]
        pltpu.make_async_copy(arrived, arrived, edge_recv.at[phase]).wait()
        swap(phase).start()

    def stage(phase):
        source = (place + 4 - phase) % 4
        for z in range(2):
            lanes = slice(z * 128, (z + 1) * 128)
            mine_z = mine[source, z * 16 : (z + 1) * 16]
            left_all[:, lanes] = mine_z[:, 16:48].reshape(512, 128)
            own = mine_z[:, 0:32].reshape(4, 2, 64, 128)
            other = theirs[source, z * 16 : (z + 1) * 16].reshape(4, 2, 64, 128)
            for half in range(2):
                right_all[:, half * 128 : half * 128 + 64, lanes] = own[:, half]
                right_all[:, half * 128 + 64 : half * 128 + 128, lanes] = other[:, half]

    arrive(0)
    for phase in range(3):
        swap(phase).wait_recv()
        stage(phase)
        for pair in range(4):
            out = dot(left_all[...], right_all[pair], 1, 1)
            total[pair] = out if phase == 0 else total[pair] + out
        arrive(phase + 1)
    swap(3).wait_recv()
    stage(3)

    for turn in (1, 2, 3, 0):
        pair = (chan // 2 + turn) % 4
        out = total[pair] + dot(left_all[...], right_all[pair], 1, 1)
        for side in range(2):
            block = out[:, side * 128 : (side + 1) * 128].reshape(16, 32, 128)
            product[pair * 2 + side] = block[:, 8:32].astype(BF16)

        def back_out(step, carry):
            d, c = (down + step // 2) % 16, pair * 2 + (chan + step) % 2

            @pl.when(d * 8 + c != here)
            def _():
                remote(
                    product.at[c, d],
                    back.at[here],
                    back_send.at[0],
                    back_recv.at[0],
                    d * 2 + core,
                    c,
                ).start()

            return carry

        lax.fori_loop(0, 32, back_out, 0)
    back[here] = product[chan, down]
    bias_weights = jnp.concatenate(
        [bias_weight_ref[...].astype(F32), jnp.zeros((8 - heads, channels), F32)], axis=0
    ).astype(BF16)
    arrived = back.at[pl.ds(0, 127)]
    pltpu.make_async_copy(arrived, arrived, back_recv.at[0]).wait()

    def add(channel, carry):
        return carry + back[channel].astype(F32)

    zero = jnp.zeros((rows, 128), F32)
    center = lax.fori_loop(0, channels, add, zero, unroll=8) * (1.0 / channels)

    def square(channel, carry):
        return carry + jnp.square(back[channel].astype(F32) - center)

    spread = lax.fori_loop(0, channels, square, zero, unroll=8) * (1.0 / channels)
    scale = lax.rsqrt(spread + 1e-05)

    def scaled(channel, carry):
        at = pl.ds(pl.multiple_of(channel * rows, 8), rows)
        norm_f[at, :] = (back[channel].astype(F32) - center) * scale
        return carry

    lax.fori_loop(0, channels, scaled, 0, unroll=8)

    right, left = (place + 1) % 4, (place + 3) % 4

    def hop(slot, g):
        whole = pl.ds(g * GROUP, GROUP)
        first = pl.ds(g * GROUP, GROUP // 2)
        second = pl.ds(g * GROUP + GROUP // 2, GROUP // 2)
        other = 1 - zone
        source, part, z, x = (
            (chan, whole, other, place),
            (chan, whole, zone, right),
            (chan, whole, zone, left),
            (other * 4 + place, whole, zone, right),
            (other * 4 + place, whole, zone, left),
            (zone * 4 + left, first, zone, right),
            (zone * 4 + right, second, zone, left),
            (other * 4 + left, first, zone, right),
            (other * 4 + right, second, zone, left),
        )[slot]
        ref = everything.at[source, part]
        return remote(ref, ref, gather_send.at[slot, g], gather_recv.at[slot, g], row, z * 4 + x)

    def relay_across(g):
        hop(0, g).wait_recv()
        hop(3, g).start()
        hop(4, g).start()
        hop(1, g).wait_recv()
        hop(5, g).start()
        hop(2, g).wait_recv()
        hop(6, g).start()

    def relay_far(g):
        hop(3, g).wait_recv()
        hop(7, g).start()
        hop(4, g).wait_recv()
        hop(8, g).start()

    def finish(g, carry):
        at = pl.ds(g * GROUP, GROUP)
        lines = []
        for t in range(GROUP):
            product_norm = norm_f[pl.ds(g * GROUP + t, channels, stride=rows), :].astype(BF16)
            out = dot(product_norm, mult_out_ref[...], 0, 0)
            a, b, c, d = (out[32 * k : 32 * k + rows] for k in range(4))
            first = core == 0
            lines.append(
                jnp.concatenate(
                    [
                        jnp.where(first, a, c),
                        jnp.where(first, c, a),
                        jnp.where(first, b, d),
                        jnp.where(first, d, b),
                    ],
                    axis=0,
                )
            )
        update = jnp.concatenate(lines, axis=0).reshape(GROUP, columns, channels)
        after = (pair_ref[at].astype(F32) + gate_f[at] * update).astype(BF16)
        after_all[at] = after
        normed = normalize(after.astype(F32), 2).astype(BF16)
        everything[chan, at] = normed
        for slot in range(3):
            hop(slot, g).start()
        padded = jnp.concatenate([normed, pad], axis=1).reshape(GROUP * 128, channels)
        bias = dot(bias_weights, padded, 1, 1)
        for t in range(GROUP):
            to = pl.ds(pl.multiple_of((g * GROUP + t) * 8, 8), 8)
            bias_f[to, :] = bias[:, t * 128 : (t + 1) * 128]
        return carry

    lax.fori_loop(0, groups, finish, 0)

    lane = lax.broadcasted_iota(jnp.int32, (rows, 128), 1)
    spare = bias_f[pl.ds(heads - 1, rows, stride=8), :]
    for h in range(heads - 1):
        line = bias_f[pl.ds(h, rows, stride=8), :]
        bias_send[h] = jnp.where(lane < columns, line, pltpu.roll(spare, columns - 32 * h, 1))
    column, part = row // 4, (row % 4) // 2
    landing = bias_mine.at[part, chan]

    def bias_out(d):
        return remote(
            bias_send, landing, bias_sem.at[0], bias_sem.at[1], d * 2 + core, column
        )

    def bias_start(step, carry):
        d = (down + step) % 16
        stays = jnp.logical_and(d == down, chan == column)

        @pl.when(stays)
        def _():
            pltpu.make_async_copy(bias_send, landing, bias_sem.at[1]).start()

        @pl.when(jnp.logical_not(stays))
        def _():
            bias_out(d).start()

        return carry

    lax.fori_loop(0, 16, bias_start, 0)
    bias_swap = remote(
        bias_mine, bias_theirs, bias_sem.at[2], bias_sem.at[3], row + 1 - 2 * core, chan
    )
    for g in range(3):
        relay_across(g)
    pltpu.make_async_copy(bias_mine, bias_mine, bias_sem.at[1]).wait()
    bias_swap.start()
    relay_far(0)
    alive = alive_ref[...] > 0.5
    pieces = 128 - columns

    def assemble(ref, side):
        for p in range(2):
            for h in range(heads):
                if h < heads - 1:
                    parts = [ref[p, c, h][:, 0:columns] for c in range(8)]
                else:
                    parts = [
                        ref[p, c, k][:, columns:128] for c in range(8) for k in range(columns // pieces)
                    ]
                line = jnp.concatenate(parts, axis=1)
                table[h, 2 * p + side] = jnp.where(alive, line * LOG2E, -1e30)

    assemble(bias_mine, core)
    bias_swap.wait_recv()
    assemble(bias_theirs, 1 - core)
    relay_far(1)

    keys = table.shape[3]
    head_of_lane = lax.broadcasted_iota(jnp.int32, (columns, channels), 1) // (channels // heads)
    score_scale = LOG2E / math.sqrt(channels // heads)
    ones = jnp.ones((keys, channels), BF16)

    def attend(g, carry):
        for slot in (5, 6, 7, 8):
            hop(slot, g).wait_recv()

        @pl.when(g + 3 < groups)
        def _():
            relay_across(g + 3)

        @pl.when(g + 2 < groups)
        def _():
            relay_far(g + 2)

        at = pl.ds(g * GROUP, GROUP)
        key_value = jnp.concatenate([key_ref[...], value_ref[...]], axis=1)
        for t in range(GROUP):
            i = g * GROUP + t
            tokens = jnp.concatenate([everything[c, i] for c in range(8)], axis=0)
            projected = dot(tokens, key_value).astype(BF16)
            key, value = projected[:, 0:channels], projected[:, channels:]
            query = dot(everything[chan, i], query_ref[...])
            split = jnp.concatenate(
                [jnp.where(head_of_lane == h, query, 0.0) for h in range(heads)], axis=0
            ).astype(BF16)
            score = dot(split, key, 1, 1) * score_scale + table[...].reshape(heads * columns, keys)
            raised = jnp.exp2(score - jnp.max(score, axis=1, keepdims=True)).astype(BF16)
            summed = dot(raised, jnp.concatenate([value, ones], axis=1))
            top = jnp.zeros((columns, channels), F32)
            bottom = jnp.ones((columns, channels), F32)
            for h in range(heads):
                mine_h = slice(h * columns, (h + 1) * columns)
                top = jnp.where(head_of_lane == h, summed[mine_h, 0:channels], top)
                bottom = jnp.where(head_of_lane == h, summed[mine_h, channels:], bottom)
            attended_f[pl.ds(t * columns, columns), :] = top / bottom

        normed = everything[chan, at].reshape(GROUP * columns, channels)
        gate = jax.nn.sigmoid(dot(normed, heads_gate_ref[...]))
        mixed = (gate * attended_f[...]).astype(BF16)
        after = after_all[at].reshape(GROUP * columns, channels).astype(F32)
        second = (after + dot(mixed, heads_out_ref[...])).astype(BF16)
        second_f = second.astype(F32)
        normed = normalize(second_f, 1).astype(BF16)
        hidden = jax.nn.silu(dot(normed, swish_ref[...])) * dot(normed, linear_ref[...])
        out = (second_f + dot(hidden.astype(BF16), project_ref[...])).astype(BF16)
        out_ref[at] = out.reshape(GROUP, columns, channels)
        return carry

    lax.fori_loop(0, groups, attend, 0)

    sent = send.at[pl.ds(0, 127)]
    pltpu.make_async_copy(sent, sent, edge_send.at[0]).wait()
    sent = back.at[pl.ds(0, 127)]
    pltpu.make_async_copy(sent, sent, back_send.at[0]).wait()
    for phase in range(4):
        swap(phase).wait_send()
    bias_swap.wait_send()

    def bias_wait(step, carry):
        d = (down + step) % 16

        @pl.when(jnp.logical_not(jnp.logical_and(d == down, chan == column)))
        def _():
            bias_out(d).wait_send()

        return carry

    lax.fori_loop(0, 16, bias_wait, 0)

    def gather_wait(g, carry):
        for slot in range(9):
            hop(slot, g).wait_send()
        return carry

    lax.fori_loop(0, groups, gather_wait, 0)


def body(
    pair_input,
    token_valid,
    left_proj,
    left_gate,
    right_proj,
    right_gate,
    mult_gate,
    mult_out,
    query_weight,
    key_weight,
    value_weight,
    bias_weight,
    heads_gate,
    heads_out,
    swish_in,
    linear_in,
    project_out,
):
    rows, columns, channels = pair_input.shape
    heads = bias_weight.shape[1]
    tokens = token_valid.shape[0]
    row, chan = lax.axis_index("row"), lax.axis_index("chan")
    validity = token_valid.astype(F32)
    row_valid = lax.dynamic_slice_in_dim(validity, row * rows, rows)
    column_valid = lax.dynamic_slice_in_dim(validity, chan * columns, columns)
    column_valid = jnp.pad(column_valid, (0, 128 - columns))
    mask = (row_valid[:, None] * column_valid[None, :]).reshape(rows, 1, 128)
    groups = rows // GROUP
    return pl.pallas_call(
        block_kernel,
        out_shape=jax.ShapeDtypeStruct((rows, columns, channels), BF16),
        in_specs=[VMEM] * 18,
        out_specs=VMEM,
        scratch_shapes=[
            pltpu.VMEM((rows * channels, 128), F32),
            pltpu.VMEM((rows * channels, 128), F32),
            pltpu.VMEM((rows, columns, channels), BF16),
            pltpu.VMEM((128, 2 * rows, 128), BF16),
            pltpu.VMEM((4, 32, 2 * rows, 128), BF16),
            pltpu.VMEM((4, 32, 32, 128), BF16),
            pltpu.VMEM((512, 256), BF16),
            pltpu.VMEM((4, 256, 256), BF16),
            pltpu.VMEM((4, 512, 256), F32),
            pltpu.VMEM((8, 16, rows, 128), BF16),
            pltpu.VMEM((128, rows, 128), BF16),
            pltpu.VMEM((rows, columns, channels), F32),
            pltpu.VMEM((channels * rows, 128), F32),
            pltpu.VMEM((rows, columns, channels), BF16),
            pltpu.VMEM((8, rows, columns, channels), BF16),
            pltpu.VMEM((rows * 8, 128), F32),
            pltpu.VMEM((heads - 1, rows, 128), F32),
            pltpu.VMEM((2, 8, heads - 1, rows, 128), F32),
            pltpu.VMEM((2, 8, heads - 1, rows, 128), F32),
            pltpu.VMEM((heads, 4, rows, tokens), F32),
            pltpu.VMEM((GROUP * columns, channels), F32),
            pltpu.SemaphoreType.DMA((1,)),
            pltpu.SemaphoreType.DMA((4,)),
            pltpu.SemaphoreType.DMA((4,)),
            pltpu.SemaphoreType.DMA((4,)),
            pltpu.SemaphoreType.DMA((1,)),
            pltpu.SemaphoreType.DMA((1,)),
            pltpu.SemaphoreType.DMA((9, groups)),
            pltpu.SemaphoreType.DMA((9, groups)),
            pltpu.SemaphoreType.DMA((4,)),
        ],
        compiler_params=pltpu.CompilerParams(
            collective_id=0, has_side_effects=True, vmem_limit_bytes=LIMIT
        ),
        name="block",
    )(
        pair_input,
        mask,
        validity.reshape(1, tokens),
        left_proj,
        left_gate,
        right_proj,
        right_gate,
        mult_gate,
        mult_out,
        query_weight,
        key_weight,
        value_weight,
        bias_weight.T,
        heads_gate,
        heads_out,
        swish_in,
        linear_in,
        project_out,
    )


def solution(mesh):
    return jax.shard_map(
        body,
        mesh=mesh,
        in_specs=(P("row", "chan", None),) + (P(),) * 16,
        out_specs=P("row", "chan", None),
        check_vma=False,
    )
```

time: 460 us -> 146 us (0.32); the launches traced: 452 us -> 145 us
  waiting for transfers between devices: 245 us -> 0 us
  Pallas kernels: 0 us -> 141 us
  matrix products: 62.7 us -> 0 us
  local copies, waits for them, and re-layouts: 51.9 us -> 3.35 us
  blocking collectives: 30.4 us -> 0 us
  other arithmetic: 25.5 us -> 0.69 us
  starting transfers between devices: 22.3 us -> 0 us
  between operations: 13.8 us -> 0.01 us
    all_gather x4 -> x0, waiting for transfers between devices: 202 us -> none  [the longest x1 102 us: body(): lax.all_gather(right_moved, 'row', axis=1, tiled=True)]
    pallas_call x0 -> x1, Pallas kernels: none -> 141 us  [body(): pl.pallas_call(block_kernel, out_shape=jax.ShapeDtypeStruct((rows, column...]
    dot_general x16 -> x0, matrix products: 62.7 us -> none  [the longest x7 16.7 us: project(): jnp.einsum('ijc,cd->ijd', inputs, matrix, preferred_element_type=jnp.floa...]
    all_to_all x2 -> x0, waiting for transfers between devices: 43.1 us -> none  [the longest x1 29.2 us: body(): lax.all_to_all(bias_rows, 'chan', split_axis=1, concat_axis=2, tiled=True)]
    all_to_all x2 -> x0, blocking collectives: 30.4 us -> none  [the longest x1 17.5 us: body(): lax.all_to_all(right_side, 'chan', split_axis=0, concat_axis=2, tiled=True)]
    all_to_all x2 -> x0, starting transfers between devices: 21.7 us -> none  [the longest x1 17.3 us: body(): lax.all_to_all(product, 'chan', split_axis=2, concat_axis=0, tiled=True)]
    reduce_sum x7 -> x0, other arithmetic: 19.7 us -> none  [the longest x1 14.5 us: body(): totals = jnp.sum(raised, axis=3)]
    unnamed x40 -> x3, local copies, waits for them, and re-layouts: 16.7 us -> 2.6 us
  transfers between devices with their start and end apart: 6 -> 0, of which waited for: 6 -> 0; matrix products, arithmetic and copies ran while one was open for 11% -> 0% of each run, Pallas kernels for 0% -> 0%
where the time goes in v2:
time: 146 us; the launch traced here: 145 us
  Pallas kernels  141 us (97%)
  local copies, waits for them, and re-layouts  3.35 us (2%)
    pallas_call x1, Pallas kernels, body(): pl.pallas_call(block_kernel, out_shape=jax.ShapeDtypeStruct((rows, column...  141 us

profile of v2, /device:TPU:1, one launch (start us, length us, event | category | flops | bytes accessed | tf_op | source)
XLA Modules:
  0.0 145.4 jit_solution(4670744619451772363)
XLA Ops:
  0.0 0.0 copy-start
  0.0 0.7 copy-done
  0.7 0.1 dynamic_slice.7
  0.8 0.1 dynamic_slice.6
  0.8 0.6 reshape.43.alive_ref
  1.4 0.7 broadcast_multiply_fusion.mask_ref
  2.1 141.4 %block.1 = bf16[24,96,128]{2,1,0:T(8,128)(2,1)} custom-call(bf16[24,96,128]{2,1,0:T(8,128)(2,1)} %pair_ref.1, f32[24,1,128]{2,1,0:T(1,128)} %broadcast_multiply_fusion.mask_ref, f32[1,768]{1,0:T(1,128)} %reshape.43.alive_ref, bf16[128,128]{1,0:T(8,128)(2,1)} %left_proj_ref.1, bf16[128,128]{1,0:T(8,128)(2,1)} %left_gate_ref.1, ...), custom_call_target="tpu_custom_call" | custom-call | tf_op jit(solution)/shard_map/block/pallas_call | solution.py:500
  143.5 1.9 %copy.19 = bf16[24,96,128]{2,1,0:T(8,128)(2,1)} copy(bf16[24,96,128]{2,1,0:T(8,128)(2,1)} %block.1) | data formatting | bytes 1179648
  (2 shorter events, 0.0 us)
Async XLA Ops:
  0.0 0.7 copy-start

commit v3 on v2

--- a/solution.py
+++ b/solution.py
@@ -43,8 +43,8 @@
 
 def block_kernel(
     pair_ref,
-    mask_ref,
-    alive_ref,
+    token_ref,
+    valid_ref,
     left_proj_ref,
     left_gate_ref,
     right_proj_ref,
@@ -67,21 +67,27 @@
     send,
     mine,
     theirs,
-    left_all,
+    left_first,
+    left_rest,
     right_all,
-    total,
-    product,
-    back,
+    product_first,
+    product_rest,
+    back_first,
+    back_rest,
     gate_f,
     norm_f,
     after_all,
     everything,
     bias_f,
-    bias_send,
-    bias_mine,
-    bias_theirs,
+    send_first,
+    send_rest,
+    mine_first,
+    mine_rest,
+    theirs_first,
+    theirs_rest,
     table,
     attended_f,
+    met_sem,
     edge_send,
     edge_recv,
     swap_send,
@@ -107,21 +113,21 @@
 
     barrier = pltpu.get_barrier_semaphore()
 
-    def greet(step):
-        d, z, x = chip(step)
-        pl.semaphore_signal(
-            barrier, inc=1, device_id=(d * 2 + core, z * 4 + x), device_id_type=MESH
-        )
-
-    pl.semaphore_signal(
-        barrier, inc=1, device_id=(row + 1 - 2 * core, chan), device_id_type=MESH
-    )
-    lax.fori_loop(1, 128, lambda step, carry: (greet(step), carry)[1], 0)
+    def signal(sem, d, c, r):
+        pl.semaphore_signal(sem, inc=1, device_id=(d * 2 + r, c), device_id_type=MESH)
+
+    signal(barrier, down, chan, 1 - core)
+    for step in range(1, 16):
+        signal(barrier, (down + step) % 16, chan, core)
+    for step in range(1, 8):
+        signal(barrier, down, (chan + step) % 8, core)
 
     weights = jnp.concatenate(
         [transposed(ref) for ref in (left_gate_ref, left_proj_ref, right_gate_ref, right_proj_ref)],
         axis=0,
     )
+
+    column_mask = valid_ref[pl.ds(chan, 1), :]
 
     def edges(g, carry):
         at = pl.ds(g * GROUP, GROUP)
@@ -131,36 +137,47 @@
         out = dot(weights, padded, 1, 1)
         for t in range(GROUP):
             lanes = slice(t * 128, (t + 1) * 128)
-            mask = mask_ref[g * GROUP + t]
+            mask = column_mask * token_ref[row * rows + g * GROUP + t].astype(F32)
             to = pl.ds(pl.multiple_of((g * GROUP + t) * channels, channels), channels)
             left_f[to, :] = mask * jax.nn.sigmoid(out[0:128, lanes]) * out[128:256, lanes]
             right_f[to, :] = mask * jax.nn.sigmoid(out[256:384, lanes]) * out[384:512, lanes]
         return carry
 
-    lax.fori_loop(0, groups, edges, 0)
-    pl.semaphore_wait(barrier, 128)
+    lax.fori_loop(0, groups // 2, edges, 0)
+    pl.semaphore_wait(barrier, 23)
+    for step in range(1, 8):
+        signal(met_sem, down, (chan + step) % 8, core)
+    lax.fori_loop(groups // 2, groups, edges, 0)
+    pl.semaphore_wait(met_sem, 7)
 
     def edge_block(channel):
         at = pl.ds(channel, rows, stride=channels)
         return jnp.concatenate([right_f[at, :], left_f[at, :]], axis=0).astype(BF16)
+
+    def edge_copy(step, part):
+        d, z, x = chip(step)
+        channel = d * 8 + z * 4 + x
+        at = pl.ds(0, 32) if part == 0 else pl.ds(32, 16)
+        phase = step // 32 if part == 0 else 4
+        return remote(
+            send.at[channel, at],
+            mine.at[place, zone * 16 + down, at],
+            edge_send.at[0],
+            edge_recv.at[phase],
+            d * 2 + core,
+            z * 4 + x,
+        )
 
     def edge_out(step, carry):
         d, z, x = chip(step)
         channel = d * 8 + z * 4 + x
         send[channel] = edge_block(channel)
-        phase = step // 32
-        remote(
-            send.at[channel],
-            mine.at[place, zone * 16 + down],
-            edge_send.at[0],
-            edge_recv.at[phase],
-            d * 2 + core,
-            z * 4 + x,
-        ).start()
+        edge_copy(step, 0).start()
         return carry
 
     lax.fori_loop(1, 128, edge_out, 0)
     mine[place, zone * 16 + down] = edge_block(here)
+    lax.fori_loop(1, 128, lambda step, carry: (edge_copy(step, 1).start(), carry)[1], 0)
 
     def gates(g, carry):
         at = pl.ds(g * GROUP, GROUP)
@@ -184,39 +201,37 @@
 
     def arrive(phase):
         count = 31 if phase == 0 else 32
-        arrived = mine.at[0, pl.ds(0, count)]
+        arrived = mine.at[0, pl.ds(0, count), pl.ds(0, 32)]
         pltpu.make_async_copy(arrived, arrived, edge_recv.at[phase]).wait()
         swap(phase).start()
 
     def stage(phase):
         source = (place + 4 - phase) % 4
         for z in range(2):
-            lanes = slice(z * 128, (z + 1) * 128)
-            mine_z = mine[source, z * 16 : (z + 1) * 16]
-            left_all[:, lanes] = mine_z[:, 16:48].reshape(512, 128)
-            own = mine_z[:, 0:32].reshape(4, 2, 64, 128)
+            lanes = slice(phase * 256 + z * 128, phase * 256 + (z + 1) * 128)
+            mine_z = mine[source, z * 16 : (z + 1) * 16, 0:32, :]
+            left_first[:, lanes] = mine_z.astype(F32)[:, 24:32].reshape(128, 128).astype(BF16)
+            own = mine_z.reshape(4, 2, 64, 128)
             other = theirs[source, z * 16 : (z + 1) * 16].reshape(4, 2, 64, 128)
             for half in range(2):
                 right_all[:, half * 128 : half * 128 + 64, lanes] = own[:, half]
                 right_all[:, half * 128 + 64 : half * 128 + 128, lanes] = other[:, half]
 
-    arrive(0)
-    for phase in range(3):
-        swap(phase).wait_recv()
-        stage(phase)
-        for pair in range(4):
-            out = dot(left_all[...], right_all[pair], 1, 1)
-            total[pair] = out if phase == 0 else total[pair] + out
-        arrive(phase + 1)
+    for phase in range(4):
+        arrive(phase)
+        if phase > 0:
+            swap(phase - 1).wait_recv()
+            stage(phase - 1)
     swap(3).wait_recv()
     stage(3)
 
-    for turn in (1, 2, 3, 0):
+    def multiply(left, product, back, part, turn):
         pair = (chan // 2 + turn) % 4
-        out = total[pair] + dot(left_all[...], right_all[pair], 1, 1)
+        count = product.shape[2]
+        out = dot(left[...], right_all[pair], 1, 1)
         for side in range(2):
-            block = out[:, side * 128 : (side + 1) * 128].reshape(16, 32, 128)
-            product[pair * 2 + side] = block[:, 8:32].astype(BF16)
+            block = out[:, side * 128 : (side + 1) * 128].reshape(16, count, 128)
+            product[pair * 2 + side] = block.astype(BF16)
 
         def back_out(step, carry):
             d, c = (down + step // 2) % 16, pair * 2 + (chan + step) % 2
@@ -226,8 +241,8 @@
                 remote(
                     product.at[c, d],
                     back.at[here],
-                    back_send.at[0],
-                    back_recv.at[0],
+                    back_send.at[part],
+                    back_recv.at[part],
                     d * 2 + core,
                     c,
                 ).start()
@@ -235,31 +250,47 @@
             return carry
 
         lax.fori_loop(0, 32, back_out, 0)
-    back[here] = product[chan, down]
+
+    for turn in (1, 2, 3, 0):
+        multiply(left_first, product_first, back_first, 0, turn)
+    back_first[here] = product_first[chan, down]
+    arrived = back_rest.at[pl.ds(0, 127)]
+    pltpu.make_async_copy(arrived, arrived, edge_recv.at[4]).wait()
+    for phase in range(4):
+        source = (place + 4 - phase) % 4
+        for z in range(2):
+            lanes = slice(phase * 256 + z * 128, phase * 256 + (z + 1) * 128)
+            left_rest[:, lanes] = mine[source, z * 16 : (z + 1) * 16, 32:48, :].reshape(256, 128)
+    for turn in (1, 2, 3, 0):
+        multiply(left_rest, product_rest, back_rest, 1, turn)
+    back_rest[here] = product_rest[chan, down]
     bias_weights = jnp.concatenate(
         [bias_weight_ref[...].astype(F32), jnp.zeros((8 - heads, channels), F32)], axis=0
     ).astype(BF16)
-    arrived = back.at[pl.ds(0, 127)]
-    pltpu.make_async_copy(arrived, arrived, back_recv.at[0]).wait()
-
-    def add(channel, carry):
-        return carry + back[channel].astype(F32)
-
-    zero = jnp.zeros((rows, 128), F32)
-    center = lax.fori_loop(0, channels, add, zero, unroll=8) * (1.0 / channels)
-
-    def square(channel, carry):
-        return carry + jnp.square(back[channel].astype(F32) - center)
-
-    spread = lax.fori_loop(0, channels, square, zero, unroll=8) * (1.0 / channels)
-    scale = lax.rsqrt(spread + 1e-05)
-
-    def scaled(channel, carry):
-        at = pl.ds(pl.multiple_of(channel * rows, 8), rows)
-        norm_f[at, :] = (back[channel].astype(F32) - center) * scale
-        return carry
-
-    lax.fori_loop(0, channels, scaled, 0, unroll=8)
+
+    def product_norms(back, part):
+        count = back.shape[1]
+        arrived = back.at[pl.ds(0, 127)]
+        pltpu.make_async_copy(arrived, arrived, back_recv.at[part]).wait()
+
+        def add(channel, carry):
+            return carry + back[channel].astype(F32)
+
+        zero = jnp.zeros((count, 128), F32)
+        center = lax.fori_loop(0, channels, add, zero, unroll=8) * (1.0 / channels)
+
+        def square(channel, carry):
+            return carry + jnp.square(back[channel].astype(F32) - center)
+
+        spread = lax.fori_loop(0, channels, square, zero, unroll=8) * (1.0 / channels)
+        scale = lax.rsqrt(spread + 1e-05)
+
+        def scaled(channel, carry):
+            at = pl.ds(pl.multiple_of(channel * count, 8), count)
+            norm_f[at, :] = (back[channel].astype(F32) - center) * scale
+            return carry
+
+        lax.fori_loop(0, channels, scaled, 0, unroll=8)
 
     right, left = (place + 1) % 4, (place + 3) % 4
 
@@ -297,11 +328,12 @@
         hop(4, g).wait_recv()
         hop(8, g).start()
 
-    def finish(g, carry):
+    def finish(g, first_row, count):
         at = pl.ds(g * GROUP, GROUP)
         lines = []
         for t in range(GROUP):
-            product_norm = norm_f[pl.ds(g * GROUP + t, channels, stride=rows), :].astype(BF16)
+            line = norm_f[pl.ds(g * GROUP + t - first_row, channels, stride=count), :]
+            product_norm = line.astype(BF16)
             out = dot(product_norm, mult_out_ref[...], 0, 0)
             a, b, c, d = (out[32 * k : 32 * k + rows] for k in range(4))
             first = core == 0
@@ -328,65 +360,117 @@
         for t in range(GROUP):
             to = pl.ds(pl.multiple_of((g * GROUP + t) * 8, 8), 8)
             bias_f[to, :] = bias[:, t * 128 : (t + 1) * 128]
-        return carry
-
-    lax.fori_loop(0, groups, finish, 0)
-
-    lane = lax.broadcasted_iota(jnp.int32, (rows, 128), 1)
-    spare = bias_f[pl.ds(heads - 1, rows, stride=8), :]
-    for h in range(heads - 1):
-        line = bias_f[pl.ds(h, rows, stride=8), :]
-        bias_send[h] = jnp.where(lane < columns, line, pltpu.roll(spare, columns - 32 * h, 1))
-    column, part = row // 4, (row % 4) // 2
-    landing = bias_mine.at[part, chan]
-
-    def bias_out(d):
+
+    column, half_of_four = row // 4, (row % 4) // 2
+    pieces = 128 - columns
+
+    def bias_copy(refs, part, d):
         return remote(
-            bias_send, landing, bias_sem.at[0], bias_sem.at[1], d * 2 + core, column
+            refs[0],
+            refs[1].at[half_of_four, chan],
+            bias_sem.at[part, 0],
+            bias_sem.at[part, 1],
+            d * 2 + core,
+            column,
         )
 
-    def bias_start(step, carry):
-        d = (down + step) % 16
-        stays = jnp.logical_and(d == down, chan == column)
-
-        @pl.when(stays)
-        def _():
-            pltpu.make_async_copy(bias_send, landing, bias_sem.at[1]).start()
-
-        @pl.when(jnp.logical_not(stays))
-        def _():
-            bias_out(d).start()
-
-        return carry
-
-    lax.fori_loop(0, 16, bias_start, 0)
-    bias_swap = remote(
-        bias_mine, bias_theirs, bias_sem.at[2], bias_sem.at[3], row + 1 - 2 * core, chan
-    )
-    for g in range(3):
-        relay_across(g)
-    pltpu.make_async_copy(bias_mine, bias_mine, bias_sem.at[1]).wait()
-    bias_swap.start()
-    relay_far(0)
-    alive = alive_ref[...] > 0.5
-    pieces = 128 - columns
-
-    def assemble(ref, side):
+    def stays(d):
+        return jnp.logical_and(d == down, chan == column)
+
+    def bias_out(refs, part, first_row):
+        count = refs[0].shape[1]
+        lane = lax.broadcasted_iota(jnp.int32, (count, 128), 1)
+        spare = bias_f[pl.ds(first_row * 8 + heads - 1, count, stride=8), :]
+        for h in range(heads - 1):
+            line = bias_f[pl.ds(first_row * 8 + h, count, stride=8), :]
+            refs[0][h] = jnp.where(lane < columns, line, pltpu.roll(spare, columns - pieces * h, 1))
+
+        def start(step, carry):
+            d = (down + step) % 16
+
+            @pl.when(stays(d))
+            def _():
+                pltpu.make_async_copy(
+                    refs[0], refs[1].at[half_of_four, chan], bias_sem.at[part, 1]
+                ).start()
+
+            @pl.when(jnp.logical_not(stays(d)))
+            def _():
+                bias_copy(refs, part, d).start()
+
+            return carry
+
+        lax.fori_loop(0, 16, start, 0)
+
+    def bias_drain(refs, part):
+        def wait(step, carry):
+            d = (down + step) % 16
+
+            @pl.when(jnp.logical_not(stays(d)))
+            def _():
+                bias_copy(refs, part, d).wait_send()
+
+            return carry
+
+        lax.fori_loop(0, 16, wait, 0)
+
+    def bias_swap(refs, part):
+        return remote(
+            refs[1], refs[2], bias_sem.at[part, 2], bias_sem.at[part, 3], row + 1 - 2 * core, chan
+        )
+
+    def bias_arrive(refs, part):
+        pltpu.make_async_copy(refs[1], refs[1], bias_sem.at[part, 1]).wait()
+        bias_swap(refs, part).start()
+
+    alive = jnp.concatenate([valid_ref[c : c + 1, 0:columns] for c in range(8)], axis=1) > 0.5
+
+    def assemble(ref, side, first_row):
+        count = ref.shape[3]
         for p in range(2):
             for h in range(heads):
                 if h < heads - 1:
                     parts = [ref[p, c, h][:, 0:columns] for c in range(8)]
                 else:
                     parts = [
-                        ref[p, c, k][:, columns:128] for c in range(8) for k in range(columns // pieces)
+                        ref[p, c, k][:, columns:128]
+                        for c in range(8)
+                        for k in range(columns // pieces)
                     ]
                 line = jnp.concatenate(parts, axis=1)
-                table[h, 2 * p + side] = jnp.where(alive, line * LOG2E, -1e30)
-
-    assemble(bias_mine, core)
-    bias_swap.wait_recv()
-    assemble(bias_theirs, 1 - core)
+                table[h, 2 * p + side, first_row : first_row + count] = jnp.where(
+                    alive, line * LOG2E, -1e30
+                )
+
+    early = (send_first, mine_first, theirs_first)
+    late = (send_rest, mine_rest, theirs_rest)
+    early_rows, late_rows = send_first.shape[1], send_rest.shape[1]
+    early_groups = early_rows // GROUP
+
+    product_norms(back_first, 0)
+    for g in range(early_groups):
+        finish(g, 0, early_rows)
+    bias_out(early, 0, 0)
+    relay_across(0)
+    relay_across(1)
+    product_norms(back_rest, 1)
+    lax.fori_loop(
+        early_groups, groups, lambda g, carry: (finish(g, early_rows, late_rows), carry)[1], 0
+    )
+    bias_out(late, 1, early_rows)
+    bias_arrive(early, 0)
+    relay_far(0)
     relay_far(1)
+    relay_across(2)
+    assemble(mine_first, core, 0)
+    bias_swap(early, 0).wait_recv()
+    assemble(theirs_first, 1 - core, 0)
+    relay_across(3)
+    bias_arrive(late, 1)
+    relay_far(2)
+    assemble(mine_rest, core, early_rows)
+    bias_swap(late, 1).wait_recv()
+    assemble(theirs_rest, 1 - core, early_rows)
 
     keys = table.shape[3]
     head_of_lane = lax.broadcasted_iota(jnp.int32, (columns, channels), 1) // (channels // heads)
@@ -397,13 +481,13 @@
         for slot in (5, 6, 7, 8):
             hop(slot, g).wait_recv()
 
+        @pl.when(g + 4 < groups)
+        def _():
+            relay_across(g + 4)
+
         @pl.when(g + 3 < groups)
         def _():
-            relay_across(g + 3)
-
-        @pl.when(g + 2 < groups)
-        def _():
-            relay_far(g + 2)
+            relay_far(g + 3)
 
         at = pl.ds(g * GROUP, GROUP)
         key_value = jnp.concatenate([key_ref[...], value_ref[...]], axis=1)
@@ -443,22 +527,13 @@
 
     sent = send.at[pl.ds(0, 127)]
     pltpu.make_async_copy(sent, sent, edge_send.at[0]).wait()
-    sent = back.at[pl.ds(0, 127)]
-    pltpu.make_async_copy(sent, sent, back_send.at[0]).wait()
+    for part, (back, refs) in enumerate(((back_first, early), (back_rest, late))):
+        sent = back.at[pl.ds(0, 127)]
+        pltpu.make_async_copy(sent, sent, back_send.at[part]).wait()
+        bias_swap(refs, part).wait_send()
+        bias_drain(refs, part)
     for phase in range(4):
         swap(phase).wait_send()
-    bias_swap.wait_send()
-
-    def bias_wait(step, carry):
-        d = (down + step) % 16
-
-        @pl.when(jnp.logical_not(jnp.logical_and(d == down, chan == column)))
-        def _():
-            bias_out(d).wait_send()
-
-        return carry
-
-    lax.fori_loop(0, 16, bias_wait, 0)
 
     def gather_wait(g, carry):
         for slot in range(9):
@@ -490,17 +565,14 @@
     rows, columns, channels = pair_input.shape
     heads = bias_weight.shape[1]
     tokens = token_valid.shape[0]
-    row, chan = lax.axis_index("row"), lax.axis_index("chan")
-    validity = token_valid.astype(F32)
-    row_valid = lax.dynamic_slice_in_dim(validity, row * rows, rows)
-    column_valid = lax.dynamic_slice_in_dim(validity, chan * columns, columns)
-    column_valid = jnp.pad(column_valid, (0, 128 - columns))
-    mask = (row_valid[:, None] * column_valid[None, :]).reshape(rows, 1, 128)
+    valid = jnp.pad(
+        token_valid.astype(F32).reshape(tokens // columns, columns), ((0, 0), (0, 128 - columns))
+    )
     groups = rows // GROUP
     return pl.pallas_call(
         block_kernel,
         out_shape=jax.ShapeDtypeStruct((rows, columns, channels), BF16),
-        in_specs=[VMEM] * 18,
+        in_specs=[VMEM, pl.BlockSpec(memory_space=pltpu.SMEM)] + [VMEM] * 16,
         out_specs=VMEM,
         scratch_shapes=[
             pltpu.VMEM((rows * channels, 128), F32),
@@ -509,30 +581,36 @@
             pltpu.VMEM((128, 2 * rows, 128), BF16),
             pltpu.VMEM((4, 32, 2 * rows, 128), BF16),
             pltpu.VMEM((4, 32, 32, 128), BF16),
-            pltpu.VMEM((512, 256), BF16),
-            pltpu.VMEM((4, 256, 256), BF16),
-            pltpu.VMEM((4, 512, 256), F32),
-            pltpu.VMEM((8, 16, rows, 128), BF16),
-            pltpu.VMEM((128, rows, 128), BF16),
+            pltpu.VMEM((128, 1024), BF16),
+            pltpu.VMEM((256, 1024), BF16),
+            pltpu.VMEM((4, 256, 1024), BF16),
+            pltpu.VMEM((8, 16, 8, 128), BF16),
+            pltpu.VMEM((8, 16, 16, 128), BF16),
+            pltpu.VMEM((128, 8, 128), BF16),
+            pltpu.VMEM((128, 16, 128), BF16),
             pltpu.VMEM((rows, columns, channels), F32),
-            pltpu.VMEM((channels * rows, 128), F32),
+            pltpu.VMEM((channels * 16, 128), F32),
             pltpu.VMEM((rows, columns, channels), BF16),
             pltpu.VMEM((8, rows, columns, channels), BF16),
             pltpu.VMEM((rows * 8, 128), F32),
-            pltpu.VMEM((heads - 1, rows, 128), F32),
-            pltpu.VMEM((2, 8, heads - 1, rows, 128), F32),
-            pltpu.VMEM((2, 8, heads - 1, rows, 128), F32),
+            pltpu.VMEM((heads - 1, 8, 128), F32),
+            pltpu.VMEM((heads - 1, 16, 128), F32),
+            pltpu.VMEM((2, 8, heads - 1, 8, 128), F32),
+            pltpu.VMEM((2, 8, heads - 1, 16, 128), F32),
+            pltpu.VMEM((2, 8, heads - 1, 8, 128), F32),
+            pltpu.VMEM((2, 8, heads - 1, 16, 128), F32),
             pltpu.VMEM((heads, 4, rows, tokens), F32),
             pltpu.VMEM((GROUP * columns, channels), F32),
+            pltpu.SemaphoreType.REGULAR,
             pltpu.SemaphoreType.DMA((1,)),
+            pltpu.SemaphoreType.DMA((5,)),
             pltpu.SemaphoreType.DMA((4,)),
             pltpu.SemaphoreType.DMA((4,)),
-            pltpu.SemaphoreType.DMA((4,)),
-            pltpu.SemaphoreType.DMA((1,)),
-            pltpu.SemaphoreType.DMA((1,)),
+            pltpu.SemaphoreType.DMA((2,)),
+            pltpu.SemaphoreType.DMA((2,)),
             pltpu.SemaphoreType.DMA((9, groups)),
             pltpu.SemaphoreType.DMA((9, groups)),
-            pltpu.SemaphoreType.DMA((4,)),
+            pltpu.SemaphoreType.DMA((2, 4)),
         ],
         compiler_params=pltpu.CompilerParams(
             collective_id=0, has_side_effects=True, vmem_limit_bytes=LIMIT
@@ -540,8 +618,8 @@
         name="block",
     )(
         pair_input,
-        mask,
-        validity.reshape(1, tokens),
+        token_valid,
+        valid,
         left_proj,
         left_gate,
         right_proj,

time: 146 us -> 134 us (0.918)
  Pallas kernels: 141 us -> 130 us
    pallas_call x1, Pallas kernels: 141 us -> 130 us  [body(): pl.pallas_call(block_kernel, out_shape=jax.ShapeDtypeStruct((rows, column...]
where the time goes in v3:
time: 134 us; the launch traced here: 133 us
  Pallas kernels  130 us (97%)
  local copies, waits for them, and re-layouts  2.59 us (2%)
    pallas_call x1, Pallas kernels, body(): pl.pallas_call(block_kernel, out_shape=jax.ShapeDtypeStruct((rows, column...  130 us

profile of v3, /device:TPU:1, one launch (start us, length us, event | category | flops | bytes accessed | tf_op | source)
XLA Modules:
  0.0 133.3 jit_solution(4211569868338273096)
XLA Ops:
  0.0 0.7 convert_element_type.5
  0.7 0.1 reshape.3
  0.8 0.6 pad.4.valid_ref
  1.4 130.0 %block.1 = bf16[24,96,128]{2,1,0:T(8,128)(2,1)} custom-call(bf16[24,96,128]{2,1,0:T(8,128)(2,1)} %pair_ref.1, s32[768]{0:T(1024)} %token_ref.1, f32[8,128]{1,0:T(8,128)} %pad.4.valid_ref, bf16[128,128]{1,0:T(8,128)(2,1)} %left_proj_ref.1, bf16[128,128]{1,0:T(8,128)(2,1)} %left_gate_ref.1, bf16[128,128]{1,0:T(8,128)(2,1)} %right_proj_ref.1, ...), custom_call_target="tpu_custom_call" | custom-call | tf_op jit(solution)/shard_map/block/pallas_call | solution.py:572
  131.4 1.9 %copy.19 = bf16[24,96,128]{2,1,0:T(8,128)(2,1)} copy(bf16[24,96,128]{2,1,0:T(8,128)(2,1)} %block.1) | data formatting | bytes 1179648

commit v4 on v3

--- a/solution.py
+++ b/solution.py
@@ -64,27 +64,24 @@
     left_f,
     right_f,
     normed0,
-    send,
-    mine,
+    send_first,
+    send_rest,
+    mine_first,
+    mine_rest,
     theirs,
     left_first,
     left_rest,
     right_all,
-    product_first,
-    product_rest,
-    back_first,
-    back_rest,
+    product,
+    back,
     gate_f,
     norm_f,
     after_all,
     everything,
     bias_f,
-    send_first,
-    send_rest,
-    mine_first,
-    mine_rest,
-    theirs_first,
-    theirs_rest,
+    bias_send,
+    bias_mine,
+    bias_theirs,
     table,
     attended_f,
     met_sem,
@@ -96,7 +93,10 @@
     back_recv,
     gather_send,
     gather_recv,
-    bias_sem,
+    bias_out_sem,
+    bias_in_sem,
+    bias_swap_out,
+    bias_swap_in,
 ):
     rows, columns, channels = pair_ref.shape
     groups = rows // GROUP
@@ -150,20 +150,31 @@
     lax.fori_loop(groups // 2, groups, edges, 0)
     pl.semaphore_wait(met_sem, 7)
 
-    def edge_block(channel):
+    lane = lax.broadcasted_iota(jnp.int32, (8, 128), 1)
+    piece = 128 - columns
+
+    def edge_blocks(channel):
         at = pl.ds(channel, rows, stride=channels)
-        return jnp.concatenate([right_f[at, :], left_f[at, :]], axis=0).astype(BF16)
+        right, left = right_f[at, :], left_f[at, :]
+        packed = [
+            jnp.where(
+                lane < columns,
+                right[8 * k : 8 * k + 8],
+                pltpu.roll(left[0:8], columns - piece * k, 1),
+            )
+            for k in range(3)
+        ]
+        return jnp.concatenate(packed, axis=0).astype(BF16), left[8:rows].astype(BF16)
 
     def edge_copy(step, part):
         d, z, x = chip(step)
         channel = d * 8 + z * 4 + x
-        at = pl.ds(0, 32) if part == 0 else pl.ds(32, 16)
-        phase = step // 32 if part == 0 else 4
+        send, mine = ((send_first, mine_first), (send_rest, mine_rest))[part]
         return remote(
-            send.at[channel, at],
-            mine.at[place, zone * 16 + down, at],
-            edge_send.at[0],
-            edge_recv.at[phase],
+            send.at[channel],
+            mine.at[place, zone * 16 + down],
+            edge_send.at[part],
+            edge_recv.at[step // 32 if part == 0 else 4],
             d * 2 + core,
             z * 4 + x,
         )
@@ -171,12 +182,12 @@
     def edge_out(step, carry):
         d, z, x = chip(step)
         channel = d * 8 + z * 4 + x
-        send[channel] = edge_block(channel)
+        send_first[channel], send_rest[channel] = edge_blocks(channel)
         edge_copy(step, 0).start()
         return carry
 
     lax.fori_loop(1, 128, edge_out, 0)
-    mine[place, zone * 16 + down] = edge_block(here)
+    mine_first[place, zone * 16 + down], mine_rest[place, zone * 16 + down] = edge_blocks(here)
     lax.fori_loop(1, 128, lambda step, carry: (edge_copy(step, 1).start(), carry)[1], 0)
 
     def gates(g, carry):
@@ -191,7 +202,7 @@
     def swap(phase):
         source = (place + 4 - phase) % 4
         return remote(
-            mine.at[source, :, pl.ds(0, 32), :],
+            mine_first.at[source],
             theirs.at[source],
             swap_send.at[phase],
             swap_recv.at[phase],
@@ -200,22 +211,28 @@
         )
 
     def arrive(phase):
-        count = 31 if phase == 0 else 32
-        arrived = mine.at[0, pl.ds(0, count), pl.ds(0, 32)]
+        arrived = mine_first.at[0, pl.ds(0, 31 if phase == 0 else 32)]
         pltpu.make_async_copy(arrived, arrived, edge_recv.at[phase]).wait()
         swap(phase).start()
+
+    right_all[:, columns:128] = jnp.zeros((8, piece, 1024), BF16)
+    lanes_of = lax.broadcasted_iota(jnp.int32, (128, 128), 1)
 
     def stage(phase):
         source = (place + 4 - phase) % 4
         for z in range(2):
             lanes = slice(phase * 256 + z * 128, phase * 256 + (z + 1) * 128)
-            mine_z = mine[source, z * 16 : (z + 1) * 16, 0:32, :]
-            left_first[:, lanes] = mine_z.astype(F32)[:, 24:32].reshape(128, 128).astype(BF16)
-            own = mine_z.reshape(4, 2, 64, 128)
-            other = theirs[source, z * 16 : (z + 1) * 16].reshape(4, 2, 64, 128)
-            for half in range(2):
-                right_all[:, half * 128 : half * 128 + 64, lanes] = own[:, half]
-                right_all[:, half * 128 + 64 : half * 128 + 128, lanes] = other[:, half]
+            own = mine_first[source, z * 16 : (z + 1) * 16].astype(F32)
+            other = theirs[source, z * 16 : (z + 1) * 16].astype(F32)
+            both = jnp.concatenate([own.reshape(8, 48, 128), other.reshape(8, 48, 128)], axis=1)
+            right_all[:, 0:columns, lanes] = both.astype(BF16)
+            left = jnp.zeros((128, 128), F32)
+            for k in range(3):
+                turned = pltpu.roll(
+                    own[:, 8 * k : 8 * k + 8].reshape(128, 128), piece + piece * k, 1
+                )
+                left = jnp.where(lanes_of // piece == k, turned, left)
+            left_first[:, lanes] = left.astype(BF16)
 
     for phase in range(4):
         arrive(phase)
@@ -225,22 +242,17 @@
     swap(3).wait_recv()
     stage(3)
 
-    def multiply(left, product, back, part, turn):
+    def back_out(part, turn):
         pair = (chan // 2 + turn) % 4
-        count = product.shape[2]
-        out = dot(left[...], right_all[pair], 1, 1)
-        for side in range(2):
-            block = out[:, side * 128 : (side + 1) * 128].reshape(16, count, 128)
-            product[pair * 2 + side] = block.astype(BF16)
-
-        def back_out(step, carry):
+
+        def start(step, carry):
             d, c = (down + step // 2) % 16, pair * 2 + (chan + step) % 2
 
             @pl.when(d * 8 + c != here)
             def _():
                 remote(
-                    product.at[c, d],
-                    back.at[here],
+                    product.at[part, c, d],
+                    back.at[part, here],
                     back_send.at[part],
                     back_recv.at[part],
                     d * 2 + core,
@@ -249,45 +261,57 @@
 
             return carry
 
-        lax.fori_loop(0, 32, back_out, 0)
-
-    for turn in (1, 2, 3, 0):
-        multiply(left_first, product_first, back_first, 0, turn)
-    back_first[here] = product_first[chan, down]
-    arrived = back_rest.at[pl.ds(0, 127)]
+        lax.fori_loop(0, 32, start, 0)
+
+    def multiply(left, first_part, turn):
+        pair = (chan // 2 + turn) % 4
+        right = right_all[pl.ds(pair * 2, 2)].reshape(256, 1024)
+        out = dot(left[...], right, 1, 1)
+        for side in range(2):
+            block = out[:, side * 128 : (side + 1) * 128].reshape(16, -1, 128)
+            for k in range(block.shape[1] // 8):
+                product[first_part + k, pair * 2 + side] = block[:, 8 * k : 8 * k + 8].astype(BF16)
+        back_out(first_part, turn)
+
+    turns = (1, 2, 3, 0)
+    for turn in turns:
+        multiply(left_first, 0, turn)
+    arrived = send_rest.at[pl.ds(0, 127)]
     pltpu.make_async_copy(arrived, arrived, edge_recv.at[4]).wait()
     for phase in range(4):
         source = (place + 4 - phase) % 4
         for z in range(2):
             lanes = slice(phase * 256 + z * 128, phase * 256 + (z + 1) * 128)
-            left_rest[:, lanes] = mine[source, z * 16 : (z + 1) * 16, 32:48, :].reshape(256, 128)
-    for turn in (1, 2, 3, 0):
-        multiply(left_rest, product_rest, back_rest, 1, turn)
-    back_rest[here] = product_rest[chan, down]
+            left_rest[:, lanes] = mine_rest[source, z * 16 : (z + 1) * 16].reshape(256, 128)
+    for turn in turns:
+        multiply(left_rest, 1, turn)
+    for turn in turns:
+        back_out(2, turn)
+    for part in range(3):
+        back[part, here] = product[part, chan, down]
     bias_weights = jnp.concatenate(
         [bias_weight_ref[...].astype(F32), jnp.zeros((8 - heads, channels), F32)], axis=0
     ).astype(BF16)
 
-    def product_norms(back, part):
-        count = back.shape[1]
-        arrived = back.at[pl.ds(0, 127)]
+    def product_norms(part):
+        arrived = back.at[part, pl.ds(0, 127)]
         pltpu.make_async_copy(arrived, arrived, back_recv.at[part]).wait()
 
         def add(channel, carry):
-            return carry + back[channel].astype(F32)
-
-        zero = jnp.zeros((count, 128), F32)
+            return carry + back[part, channel].astype(F32)
+
+        zero = jnp.zeros((8, 128), F32)
         center = lax.fori_loop(0, channels, add, zero, unroll=8) * (1.0 / channels)
 
         def square(channel, carry):
-            return carry + jnp.square(back[channel].astype(F32) - center)
+            return carry + jnp.square(back[part, channel].astype(F32) - center)
 
         spread = lax.fori_loop(0, channels, square, zero, unroll=8) * (1.0 / channels)
         scale = lax.rsqrt(spread + 1e-05)
 
         def scaled(channel, carry):
-            at = pl.ds(pl.multiple_of(channel * count, 8), count)
-            norm_f[at, :] = (back[channel].astype(F32) - center) * scale
+            at = pl.ds(pl.multiple_of(channel * 8, 8), 8)
+            norm_f[at, :] = (back[part, channel].astype(F32) - center) * scale
             return carry
 
         lax.fori_loop(0, channels, scaled, 0, unroll=8)
@@ -328,14 +352,14 @@
         hop(4, g).wait_recv()
         hop(8, g).start()
 
-    def finish(g, first_row, count):
+    def finish(g):
         at = pl.ds(g * GROUP, GROUP)
         lines = []
         for t in range(GROUP):
-            line = norm_f[pl.ds(g * GROUP + t - first_row, channels, stride=count), :]
+            line = norm_f[pl.ds(g * GROUP % 8 + t, channels, stride=8), :]
             product_norm = line.astype(BF16)
             out = dot(product_norm, mult_out_ref[...], 0, 0)
-            a, b, c, d = (out[32 * k : 32 * k + rows] for k in range(4))
+            a, b, c, d = (out[rows * k : rows * k + rows] for k in range(4))
             first = core == 0
             lines.append(
                 jnp.concatenate(
@@ -361,116 +385,128 @@
             to = pl.ds(pl.multiple_of((g * GROUP + t) * 8, 8), 8)
             bias_f[to, :] = bias[:, t * 128 : (t + 1) * 128]
 
-    column, half_of_four = row // 4, (row % 4) // 2
-    pieces = 128 - columns
-
-    def bias_copy(refs, part, d):
+    column, slot_of_four = row // 4, (row % 4) // 2
+    high, low = down // 4, down % 4
+
+    def bias_copy(part, high_to):
         return remote(
-            refs[0],
-            refs[1].at[half_of_four, chan],
-            bias_sem.at[part, 0],
-            bias_sem.at[part, 1],
-            d * 2 + core,
+            bias_send.at[part],
+            bias_mine.at[part, chan % 4, slot_of_four, chan // 4],
+            bias_out_sem.at[part, 0],
+            bias_in_sem.at[part, 0],
+            (high_to * 4 + chan % 4) * 2 + core,
             column,
         )
 
-    def stays(d):
-        return jnp.logical_and(d == down, chan == column)
-
-    def bias_out(refs, part, first_row):
-        count = refs[0].shape[1]
-        lane = lax.broadcasted_iota(jnp.int32, (count, 128), 1)
-        spare = bias_f[pl.ds(first_row * 8 + heads - 1, count, stride=8), :]
+    def stays(high_to):
+        here_too = jnp.logical_and(high_to == high, chan % 4 == low)
+        return jnp.logical_and(here_too, chan == column)
+
+    def bias_out(part):
+        def line(h):
+            return bias_f[pl.ds(part * 64 + h, 8, stride=8), :]
+
         for h in range(heads - 1):
-            line = bias_f[pl.ds(first_row * 8 + h, count, stride=8), :]
-            refs[0][h] = jnp.where(lane < columns, line, pltpu.roll(spare, columns - pieces * h, 1))
-
-        def start(step, carry):
-            d = (down + step) % 16
-
-            @pl.when(stays(d))
+            spare = pltpu.roll(line(heads - 1), columns - piece * h, 1)
+            bias_send[part, h] = jnp.where(lane < columns, line(h), spare)
+        for step in range(4):
+            high_to = (high + step) % 4
+
+            @pl.when(stays(high_to))
             def _():
                 pltpu.make_async_copy(
-                    refs[0], refs[1].at[half_of_four, chan], bias_sem.at[part, 1]
+                    bias_send.at[part],
+                    bias_mine.at[part, chan % 4, slot_of_four, chan // 4],
+                    bias_in_sem.at[part, 0],
                 ).start()
 
-            @pl.when(jnp.logical_not(stays(d)))
+            @pl.when(jnp.logical_not(stays(high_to)))
             def _():
-                bias_copy(refs, part, d).start()
-
-            return carry
-
-        lax.fori_loop(0, 16, start, 0)
-
-    def bias_drain(refs, part):
-        def wait(step, carry):
-            d = (down + step) % 16
-
-            @pl.when(jnp.logical_not(stays(d)))
-            def _():
-                bias_copy(refs, part, d).wait_send()
-
-            return carry
-
-        lax.fori_loop(0, 16, wait, 0)
-
-    def bias_swap(refs, part):
+                bias_copy(part, high_to).start()
+
+    def bias_hop(part, apart):
+        ref = bias_mine.at[part, low]
         return remote(
-            refs[1], refs[2], bias_sem.at[part, 2], bias_sem.at[part, 3], row + 1 - 2 * core, chan
+            ref,
+            ref,
+            bias_out_sem.at[part, apart],
+            bias_in_sem.at[part, apart],
+            (high * 4 + (low + apart) % 4) * 2 + core,
+            chan,
         )
 
-    def bias_arrive(refs, part):
-        pltpu.make_async_copy(refs[1], refs[1], bias_sem.at[part, 1]).wait()
-        bias_swap(refs, part).start()
+    def bias_swap(part, apart):
+        source = (low + 4 - apart) % 4
+        return remote(
+            bias_mine.at[part, source],
+            bias_theirs.at[part, source],
+            bias_swap_out.at[part, apart],
+            bias_swap_in.at[part, apart],
+            row + 1 - 2 * core,
+            chan,
+        )
+
+    def bias_pass(part):
+        arrived = bias_mine.at[part, low]
+        pltpu.make_async_copy(arrived, arrived, bias_in_sem.at[part, 0]).wait()
+        for apart in (2, 1, 3):
+            bias_hop(part, apart).start()
+        bias_swap(part, 0).start()
+
+    def bias_collect(part):
+        for apart in (1, 3, 2):
+            bias_hop(part, apart).wait_recv()
+            bias_swap(part, apart).start()
 
     alive = jnp.concatenate([valid_ref[c : c + 1, 0:columns] for c in range(8)], axis=1) > 0.5
 
-    def assemble(ref, side, first_row):
-        count = ref.shape[3]
-        for p in range(2):
-            for h in range(heads):
-                if h < heads - 1:
-                    parts = [ref[p, c, h][:, 0:columns] for c in range(8)]
-                else:
-                    parts = [
-                        ref[p, c, k][:, columns:128]
-                        for c in range(8)
-                        for k in range(columns // pieces)
-                    ]
-                line = jnp.concatenate(parts, axis=1)
-                table[h, 2 * p + side, first_row : first_row + count] = jnp.where(
-                    alive, line * LOG2E, -1e30
-                )
-
-    early = (send_first, mine_first, theirs_first)
-    late = (send_rest, mine_rest, theirs_rest)
-    early_rows, late_rows = send_first.shape[1], send_rest.shape[1]
-    early_groups = early_rows // GROUP
-
-    product_norms(back_first, 0)
-    for g in range(early_groups):
-        finish(g, 0, early_rows)
-    bias_out(early, 0, 0)
+    def bias_assemble(part):
+        for apart in range(4):
+            bias_swap(part, apart).wait_recv()
+        for ref, side in ((bias_mine, core), (bias_theirs, 1 - core)):
+            for p in range(2):
+                for h in range(heads):
+                    if h < heads - 1:
+                        parts = [ref[part, c % 4, p, c // 4, h][:, 0:columns] for c in range(8)]
+                    else:
+                        parts = [
+                            ref[part, c % 4, p, c // 4, k][:, columns:128]
+                            for c in range(8)
+                            for k in range(heads - 1)
+                        ]
+                    line = jnp.concatenate(parts, axis=1)
+                    table[h, 2 * p + side, part * 8 : part * 8 + 8] = jnp.where(
+                        alive, line * LOG2E, -1e30
+                    )
+
+    product_norms(0)
+    finish(0)
+    finish(1)
+    bias_out(0)
     relay_across(0)
+    product_norms(1)
+    finish(2)
+    finish(3)
+    bias_out(1)
+    bias_pass(0)
     relay_across(1)
-    product_norms(back_rest, 1)
-    lax.fori_loop(
-        early_groups, groups, lambda g, carry: (finish(g, early_rows, late_rows), carry)[1], 0
-    )
-    bias_out(late, 1, early_rows)
-    bias_arrive(early, 0)
     relay_far(0)
+    product_norms(2)
+    finish(4)
+    finish(5)
+    bias_out(2)
+    bias_pass(1)
+    bias_collect(0)
+    relay_across(2)
     relay_far(1)
-    relay_across(2)
-    assemble(mine_first, core, 0)
-    bias_swap(early, 0).wait_recv()
-    assemble(theirs_first, 1 - core, 0)
+    bias_pass(2)
+    bias_collect(1)
+    bias_assemble(0)
     relay_across(3)
-    bias_arrive(late, 1)
     relay_far(2)
-    assemble(mine_rest, core, early_rows)
-    bias_swap(late, 1).wait_recv()
-    assemble(theirs_rest, 1 - core, early_rows)
+    bias_collect(2)
+    bias_assemble(1)
+    bias_assemble(2)
 
     keys = table.shape[3]
     head_of_lane = lax.broadcasted_iota(jnp.int32, (columns, channels), 1) // (channels // heads)
@@ -525,15 +561,24 @@
 
     lax.fori_loop(0, groups, attend, 0)
 
-    sent = send.at[pl.ds(0, 127)]
-    pltpu.make_async_copy(sent, sent, edge_send.at[0]).wait()
-    for part, (back, refs) in enumerate(((back_first, early), (back_rest, late))):
-        sent = back.at[pl.ds(0, 127)]
-        pltpu.make_async_copy(sent, sent, back_send.at[part]).wait()
-        bias_swap(refs, part).wait_send()
-        bias_drain(refs, part)
+    for part, send in enumerate((send_first, send_rest)):
+        sent = send.at[pl.ds(0, 127)]
+        pltpu.make_async_copy(sent, sent, edge_send.at[part]).wait()
     for phase in range(4):
         swap(phase).wait_send()
+    for part in range(3):
+        sent = back.at[part, pl.ds(0, 127)]
+        pltpu.make_async_copy(sent, sent, back_send.at[part]).wait()
+        for step in range(4):
+
+            @pl.when(jnp.logical_not(stays((high + step) % 4)))
+            def _():
+                bias_copy(part, (high + step) % 4).wait_send()
+
+        for apart in range(1, 4):
+            bias_hop(part, apart).wait_send()
+        for apart in range(4):
+            bias_swap(part, apart).wait_send()
 
     def gather_wait(g, carry):
         for slot in range(9):
@@ -578,39 +623,39 @@
             pltpu.VMEM((rows * channels, 128), F32),
             pltpu.VMEM((rows * channels, 128), F32),
             pltpu.VMEM((rows, columns, channels), BF16),
-            pltpu.VMEM((128, 2 * rows, 128), BF16),
-            pltpu.VMEM((4, 32, 2 * rows, 128), BF16),
-            pltpu.VMEM((4, 32, 32, 128), BF16),
+            pltpu.VMEM((128, rows, 128), BF16),
+            pltpu.VMEM((128, 16, 128), BF16),
+            pltpu.VMEM((4, 32, rows, 128), BF16),
+            pltpu.VMEM((4, 32, 16, 128), BF16),
+            pltpu.VMEM((4, 32, rows, 128), BF16),
             pltpu.VMEM((128, 1024), BF16),
             pltpu.VMEM((256, 1024), BF16),
-            pltpu.VMEM((4, 256, 1024), BF16),
-            pltpu.VMEM((8, 16, 8, 128), BF16),
-            pltpu.VMEM((8, 16, 16, 128), BF16),
-            pltpu.VMEM((128, 8, 128), BF16),
-            pltpu.VMEM((128, 16, 128), BF16),
+            pltpu.VMEM((8, 128, 1024), BF16),
+            pltpu.VMEM((3, 8, 16, 8, 128), BF16),
+            pltpu.VMEM((3, 128, 8, 128), BF16),
             pltpu.VMEM((rows, columns, channels), F32),
-            pltpu.VMEM((channels * 16, 128), F32),
+            pltpu.VMEM((channels * 8, 128), F32),
             pltpu.VMEM((rows, columns, channels), BF16),
             pltpu.VMEM((8, rows, columns, channels), BF16),
             pltpu.VMEM((rows * 8, 128), F32),
-            pltpu.VMEM((heads - 1, 8, 128), F32),
-            pltpu.VMEM((heads - 1, 16, 128), F32),
-            pltpu.VMEM((2, 8, heads - 1, 8, 128), F32),
-            pltpu.VMEM((2, 8, heads - 1, 16, 128), F32),
-            pltpu.VMEM((2, 8, heads - 1, 8, 128), F32),
-            pltpu.VMEM((2, 8, heads - 1, 16, 128), F32),
+            pltpu.VMEM((3, heads - 1, 8, 128), F32),
+            pltpu.VMEM((3, 4, 2, 2, heads - 1, 8, 128), F32),
+            pltpu.VMEM((3, 4, 2, 2, heads - 1, 8, 128), F32),
             pltpu.VMEM((heads, 4, rows, tokens), F32),
             pltpu.VMEM((GROUP * columns, channels), F32),
             pltpu.SemaphoreType.REGULAR,
-            pltpu.SemaphoreType.DMA((1,)),
+            pltpu.SemaphoreType.DMA((2,)),
             pltpu.SemaphoreType.DMA((5,)),
             pltpu.SemaphoreType.DMA((4,)),
             pltpu.SemaphoreType.DMA((4,)),
-            pltpu.SemaphoreType.DMA((2,)),
-            pltpu.SemaphoreType.DMA((2,)),
+            pltpu.SemaphoreType.DMA((3,)),
+            pltpu.SemaphoreType.DMA((3,)),
             pltpu.SemaphoreType.DMA((9, groups)),
             pltpu.SemaphoreType.DMA((9, groups)),
-            pltpu.SemaphoreType.DMA((2, 4)),
+            pltpu.SemaphoreType.DMA((3, 4)),
+            pltpu.SemaphoreType.DMA((3, 4)),
+            pltpu.SemaphoreType.DMA((3, 4)),
+            pltpu.SemaphoreType.DMA((3, 4)),
         ],
         compiler_params=pltpu.CompilerParams(
             collective_id=0, has_side_effects=True, vmem_limit_bytes=LIMIT

time: 134 us -> 121 us (0.903)
  Pallas kernels: 130 us -> 118 us
    pallas_call x1, Pallas kernels: 130 us -> 118 us  [body(): pl.pallas_call(block_kernel, out_shape=jax.ShapeDtypeStruct((rows, column...]
where the time goes in v4:
time: 121 us
  Pallas kernels  118 us (98%)
  local copies, waits for them, and re-layouts  2.59 us (2%)
    pallas_call x1, Pallas kernels, body(): pl.pallas_call(block_kernel, out_shape=jax.ShapeDtypeStruct((rows, column...  118 us

profile of v4, /device:TPU:1, one launch (start us, length us, event | category | flops | bytes accessed | tf_op | source)
XLA Modules:
  0.0 120.9 jit_solution(9739586549279456486)
XLA Ops:
  0.0 0.7 convert_element_type.5
  0.7 0.1 reshape.3
  0.8 0.6 pad.4.valid_ref
  1.4 117.6 %block.1 = bf16[24,96,128]{2,1,0:T(8,128)(2,1)} custom-call(bf16[24,96,128]{2,1,0:T(8,128)(2,1)} %pair_ref.1, s32[768]{0:T(1024)} %token_ref.1, f32[8,128]{1,0:T(8,128)} %pad.4.valid_ref, bf16[128,128]{1,0:T(8,128)(2,1)} %left_proj_ref.1, bf16[128,128]{1,0:T(8,128)(2,1)} %left_gate_ref.1, bf16[128,128]{1,0:T(8,128)(2,1)} %right_proj_ref.1, ...), custom_call_target="tpu_custom_call" | custom-call | tf_op jit(solution)/shard_map/block/pallas_call | solution.py:617
  119.0 1.9 %copy.19 = bf16[24,96,128]{2,1,0:T(8,128)(2,1)} copy(bf16[24,96,128]{2,1,0:T(8,128)(2,1)} %block.1) | data formatting | bytes 1179648

commit v5 on v4

--- a/solution.py
+++ b/solution.py
@@ -127,7 +127,8 @@
         axis=0,
     )
 
-    column_mask = valid_ref[pl.ds(chan, 1), :]
+    valid = jnp.broadcast_to(valid_ref[...].reshape(1, 768).astype(F32), (8, 768))
+    column_mask = pltpu.roll(valid, (768 - columns * chan) % 768, 1)[0:1, 0:128]
 
     def edges(g, carry):
         at = pl.ds(g * GROUP, GROUP)
@@ -143,12 +144,10 @@
             right_f[to, :] = mask * jax.nn.sigmoid(out[256:384, lanes]) * out[384:512, lanes]
         return carry
 
-    lax.fori_loop(0, groups // 2, edges, 0)
+    lax.fori_loop(0, groups, edges, 0)
     pl.semaphore_wait(barrier, 23)
     for step in range(1, 8):
         signal(met_sem, down, (chan + step) % 8, core)
-    lax.fori_loop(groups // 2, groups, edges, 0)
-    pl.semaphore_wait(met_sem, 7)
 
     lane = lax.broadcasted_iota(jnp.int32, (8, 128), 1)
     piece = 128 - columns
@@ -186,7 +185,9 @@
         edge_copy(step, 0).start()
         return carry
 
-    lax.fori_loop(1, 128, edge_out, 0)
+    lax.fori_loop(1, 16, edge_out, 0)
+    pl.semaphore_wait(met_sem, 7)
+    lax.fori_loop(16, 128, edge_out, 0)
     mine_first[place, zone * 16 + down], mine_rest[place, zone * 16 + down] = edge_blocks(here)
     lax.fori_loop(1, 128, lambda step, carry: (edge_copy(step, 1).start(), carry)[1], 0)
 
@@ -316,28 +317,27 @@
 
         lax.fori_loop(0, channels, scaled, 0, unroll=8)
 
-    right, left = (place + 1) % 4, (place + 3) % 4
+    right, left, opposite = (place + 1) % 4, (place + 3) % 4, (place + 2) % 4
+    far_zone = 1 - zone
 
     def hop(slot, g):
         whole = pl.ds(g * GROUP, GROUP)
         first = pl.ds(g * GROUP, GROUP // 2)
         second = pl.ds(g * GROUP + GROUP // 2, GROUP // 2)
-        other = 1 - zone
         source, part, z, x = (
-            (chan, whole, other, place),
+            (chan, whole, far_zone, place),
             (chan, whole, zone, right),
             (chan, whole, zone, left),
-            (other * 4 + place, whole, zone, right),
-            (other * 4 + place, whole, zone, left),
+            (far_zone * 4 + place, whole, zone, right),
+            (far_zone * 4 + place, whole, zone, left),
             (zone * 4 + left, first, zone, right),
             (zone * 4 + right, second, zone, left),
-            (other * 4 + left, first, zone, right),
-            (other * 4 + right, second, zone, left),
+            (zone * 4 + opposite, whole, far_zone, place),
         )[slot]
         ref = everything.at[source, part]
         return remote(ref, ref, gather_send.at[slot, g], gather_recv.at[slot, g], row, z * 4 + x)
 
-    def relay_across(g):
+    def relay(g):
         hop(0, g).wait_recv()
         hop(3, g).start()
         hop(4, g).start()
@@ -346,11 +346,10 @@
         hop(2, g).wait_recv()
         hop(6, g).start()
 
-    def relay_far(g):
-        hop(3, g).wait_recv()
+    def relay_back(g):
+        hop(5, g).wait_recv()
+        hop(6, g).wait_recv()
         hop(7, g).start()
-        hop(4, g).wait_recv()
-        hop(8, g).start()
 
     def finish(g):
         at = pl.ds(g * GROUP, GROUP)
@@ -458,7 +457,7 @@
             bias_hop(part, apart).wait_recv()
             bias_swap(part, apart).start()
 
-    alive = jnp.concatenate([valid_ref[c : c + 1, 0:columns] for c in range(8)], axis=1) > 0.5
+    alive = valid[0:1] > 0.5
 
     def bias_assemble(part):
         for apart in range(4):
@@ -483,28 +482,29 @@
     finish(0)
     finish(1)
     bias_out(0)
-    relay_across(0)
+    relay(0)
     product_norms(1)
     finish(2)
     finish(3)
     bias_out(1)
     bias_pass(0)
-    relay_across(1)
-    relay_far(0)
+    relay(1)
     product_norms(2)
     finish(4)
     finish(5)
     bias_out(2)
     bias_pass(1)
     bias_collect(0)
-    relay_across(2)
-    relay_far(1)
+    relay(2)
+    relay(3)
     bias_pass(2)
     bias_collect(1)
     bias_assemble(0)
-    relay_across(3)
-    relay_far(2)
+    relay_back(0)
+    relay(4)
     bias_collect(2)
+    relay(5)
+    relay_back(1)
     bias_assemble(1)
     bias_assemble(2)
 
@@ -514,16 +514,12 @@
     ones = jnp.ones((keys, channels), BF16)
 
     def attend(g, carry):
-        for slot in (5, 6, 7, 8):
+        for slot in (3, 4, 7):
             hop(slot, g).wait_recv()
 
-        @pl.when(g + 4 < groups)
+        @pl.when(g + 2 < groups)
         def _():
-            relay_across(g + 4)
-
-        @pl.when(g + 3 < groups)
-        def _():
-            relay_far(g + 3)
+            relay_back(g + 2)
 
         at = pl.ds(g * GROUP, GROUP)
         key_value = jnp.concatenate([key_ref[...], value_ref[...]], axis=1)
@@ -581,7 +577,7 @@
             bias_swap(part, apart).wait_send()
 
     def gather_wait(g, carry):
-        for slot in range(9):
+        for slot in range(8):
             hop(slot, g).wait_send()
         return carry
 
@@ -610,9 +606,6 @@
     rows, columns, channels = pair_input.shape
     heads = bias_weight.shape[1]
     tokens = token_valid.shape[0]
-    valid = jnp.pad(
-        token_valid.astype(F32).reshape(tokens // columns, columns), ((0, 0), (0, 128 - columns))
-    )
     groups = rows // GROUP
     return pl.pallas_call(
         block_kernel,
@@ -650,8 +643,8 @@
             pltpu.SemaphoreType.DMA((4,)),
             pltpu.SemaphoreType.DMA((3,)),
             pltpu.SemaphoreType.DMA((3,)),
-            pltpu.SemaphoreType.DMA((9, groups)),
-            pltpu.SemaphoreType.DMA((9, groups)),
+            pltpu.SemaphoreType.DMA((8, groups)),
+            pltpu.SemaphoreType.DMA((8, groups)),
             pltpu.SemaphoreType.DMA((3, 4)),
             pltpu.SemaphoreType.DMA((3, 4)),
             pltpu.SemaphoreType.DMA((3, 4)),
@@ -664,7 +657,7 @@
     )(
         pair_input,
         token_valid,
-        valid,
+        token_valid,
         left_proj,
         left_gate,
         right_proj,

time: 121 us -> 116 us (0.959)
  Pallas kernels: 118 us -> 114 us
    pallas_call x1, Pallas kernels: 118 us -> 114 us  [body(): pl.pallas_call(block_kernel, out_shape=jax.ShapeDtypeStruct((rows, column...]
where the time goes in v5:
time: 116 us
  Pallas kernels  114 us (98%)
  local copies, waits for them, and re-layouts  1.92 us (2%)
    pallas_call x1, Pallas kernels, body(): pl.pallas_call(block_kernel, out_shape=jax.ShapeDtypeStruct((rows, column...  114 us

profile of v5, /device:TPU:1, one launch (start us, length us, event | category | flops | bytes accessed | tf_op | source)
XLA Modules:
  0.0 116.2 jit_solution(17912443636657291362)
XLA Ops:
  0.0 114.3 %block.1 = bf16[24,96,128]{2,1,0:T(8,128)(2,1)} custom-call(bf16[24,96,128]{2,1,0:T(8,128)(2,1)} %pair_ref.1, s32[768]{0:T(1024)} %valid_ref.1, s32[768]{0:T(1024)} %valid_ref.1, bf16[128,128]{1,0:T(8,128)(2,1)} %left_proj_ref.1, bf16[128,128]{1,0:T(8,128)(2,1)} %left_gate_ref.1, bf16[128,128]{1,0:T(8,128)(2,1)} %right_proj_ref.1, ...), custom_call_target="tpu_custom_call" | custom-call | tf_op jit(solution)/shard_map/block/pallas_call | solution.py:610
  114.3 1.9 %copy.19 = bf16[24,96,128]{2,1,0:T(8,128)(2,1)} copy(bf16[24,96,128]{2,1,0:T(8,128)(2,1)} %block.1) | data formatting | bytes 1179648

commit v6 on v5

--- a/solution.py
+++ b/solution.py
@@ -337,10 +337,16 @@
         ref = everything.at[source, part]
         return remote(ref, ref, gather_send.at[slot, g], gather_recv.at[slot, g], row, z * 4 + x)
 
-    def relay(g):
+    def launch(g):
+        for slot in range(3):
+            hop(slot, g).start()
+
+    def relay_zone(g):
         hop(0, g).wait_recv()
         hop(3, g).start()
         hop(4, g).start()
+
+    def relay_ring(g):
         hop(1, g).wait_recv()
         hop(5, g).start()
         hop(2, g).wait_recv()
@@ -376,8 +382,6 @@
         after_all[at] = after
         normed = normalize(after.astype(F32), 2).astype(BF16)
         everything[chan, at] = normed
-        for slot in range(3):
-            hop(slot, g).start()
         padded = jnp.concatenate([normed, pad], axis=1).reshape(GROUP * 128, channels)
         bias = dot(bias_weights, padded, 1, 1)
         for t in range(GROUP):
@@ -481,32 +485,41 @@
     product_norms(0)
     finish(0)
     finish(1)
+    launch(0)
+    launch(1)
     bias_out(0)
-    relay(0)
     product_norms(1)
     finish(2)
     finish(3)
+    launch(2)
+    launch(3)
     bias_out(1)
     bias_pass(0)
-    relay(1)
+    relay_ring(0)
+    relay_zone(0)
     product_norms(2)
     finish(4)
     finish(5)
     bias_out(2)
+    launch(4)
+    launch(5)
     bias_pass(1)
+    relay_zone(1)
+    relay_ring(1)
     bias_collect(0)
-    relay(2)
-    relay(3)
     bias_pass(2)
     bias_collect(1)
+    relay_zone(2)
+    relay_ring(2)
     bias_assemble(0)
+    bias_assemble(1)
     relay_back(0)
-    relay(4)
+    relay_zone(3)
     bias_collect(2)
-    relay(5)
+    bias_assemble(2)
+    relay_ring(3)
+    relay_zone(4)
     relay_back(1)
-    bias_assemble(1)
-    bias_assemble(2)
 
     keys = table.shape[3]
     head_of_lane = lax.broadcasted_iota(jnp.int32, (columns, channels), 1) // (channels // heads)
@@ -514,6 +527,15 @@
     ones = jnp.ones((keys, channels), BF16)
 
     def attend(g, carry):
+        @pl.when(g == 0)
+        def _():
+            relay_zone(groups - 1)
+            relay_ring(groups - 2)
+
+        @pl.when(g == 1)
+        def _():
+            relay_ring(groups - 1)
+
         for slot in (3, 4, 7):
             hop(slot, g).wait_recv()
 

time: 116 us -> 112 us (0.966)
  Pallas kernels: 114 us -> 110 us
    pallas_call x1, Pallas kernels: 114 us -> 110 us  [body(): pl.pallas_call(block_kernel, out_shape=jax.ShapeDtypeStruct((rows, column...]
where the time goes in v6:
time: 112 us
  Pallas kernels  110 us (98%)
  local copies, waits for them, and re-layouts  1.92 us (2%)
    pallas_call x1, Pallas kernels, body(): pl.pallas_call(block_kernel, out_shape=jax.ShapeDtypeStruct((rows, column...  110 us

profile of v6, /device:TPU:1, one launch (start us, length us, event | category | flops | bytes accessed | tf_op | source)
XLA Modules:
  0.0 111.9 jit_solution(1016348006625652381)
XLA Ops:
  0.0 109.9 %block.1 = bf16[24,96,128]{2,1,0:T(8,128)(2,1)} custom-call(bf16[24,96,128]{2,1,0:T(8,128)(2,1)} %pair_ref.1, s32[768]{0:T(1024)} %valid_ref.1, s32[768]{0:T(1024)} %valid_ref.1, bf16[128,128]{1,0:T(8,128)(2,1)} %left_proj_ref.1, bf16[128,128]{1,0:T(8,128)(2,1)} %left_gate_ref.1, bf16[128,128]{1,0:T(8,128)(2,1)} %right_proj_ref.1, ...), custom_call_target="tpu_custom_call" | custom-call | tf_op jit(solution)/shard_map/block/pallas_call | solution.py:632
  109.9 1.9 %copy.19 = bf16[24,96,128]{2,1,0:T(8,128)(2,1)} copy(bf16[24,96,128]{2,1,0:T(8,128)(2,1)} %block.1) | data formatting | bytes 1179648

commit v7 on v6

--- a/solution.py
+++ b/solution.py
@@ -144,10 +144,11 @@
             right_f[to, :] = mask * jax.nn.sigmoid(out[256:384, lanes]) * out[384:512, lanes]
         return carry
 
-    lax.fori_loop(0, groups, edges, 0)
+    lax.fori_loop(0, groups // 2, edges, 0)
     pl.semaphore_wait(barrier, 23)
     for step in range(1, 8):
         signal(met_sem, down, (chan + step) % 8, core)
+    lax.fori_loop(groups // 2, groups, edges, 0)
 
     lane = lax.broadcasted_iota(jnp.int32, (8, 128), 1)
     piece = 128 - columns

time: 112 us -> 113 us (level); the launches traced: 112 us -> 112 us
  no operation moved by 1% of the time
where the time goes in v7:
time: 113 us; the launch traced here: 112 us
  Pallas kernels  110 us (97%)
  local copies, waits for them, and re-layouts  1.92 us (2%)
    pallas_call x1, Pallas kernels, body(): pl.pallas_call(block_kernel, out_shape=jax.ShapeDtypeStruct((rows, column...  110 us

profile of v7, /device:TPU:1, one launch (start us, length us, event | category | flops | bytes accessed | tf_op | source)
XLA Modules:
  0.0 111.7 jit_solution(10851508019986368712)
XLA Ops:
  0.0 109.8 %block.1 = bf16[24,96,128]{2,1,0:T(8,128)(2,1)} custom-call(bf16[24,96,128]{2,1,0:T(8,128)(2,1)} %pair_ref.1, s32[768]{0:T(1024)} %valid_ref.1, s32[768]{0:T(1024)} %valid_ref.1, bf16[128,128]{1,0:T(8,128)(2,1)} %left_proj_ref.1, bf16[128,128]{1,0:T(8,128)(2,1)} %left_gate_ref.1, bf16[128,128]{1,0:T(8,128)(2,1)} %right_proj_ref.1, ...), custom_call_target="tpu_custom_call" | custom-call | tf_op jit(solution)/shard_map/block/pallas_call | solution.py:633
  109.8 1.9 %copy.19 = bf16[24,96,128]{2,1,0:T(8,128)(2,1)} copy(bf16[24,96,128]{2,1,0:T(8,128)(2,1)} %block.1) | data formatting | bytes 1179648
